TPU v7x, 32 devices: a whole 2x2x4 slice. The times are simulated.
32 devices in a mesh: dp: 8 (over y, x, core), tensor: 4 (over z).
Axes of the slice: x: 2, y: 2, z: 4, core: 2. Of those that a mesh axis runs over, the one named last changes fastest.
Arguments:
- gen_tokens: bfloat16 [24, 5, 256, 512], P('dp', None, 'tensor'), may hold values from -6 to 6
- rec_grad: bfloat16 [24, 5, 256, 512], P('dp', None, 'tensor'), may hold values from -6 to 6
- adv_grad: bfloat16 [24, 5, 256, 512], P('dp', None, 'tensor'), may hold values from -6 to 6
- gen_aspect: int32 [24], P('dp'), may hold values from 0 to 2
- gen_frames: int32 [24], P('dp'), may hold values from 1 to 5, 90 in all
- disc_tokens: bfloat16 [24, 5, 256, 512], P('dp', None, 'tensor'), may hold values from -6 to 6
- disc_aspect: int32 [24], P('dp'), may hold values from 0 to 2
- disc_frames: int32 [24], P('dp'), may hold values from 1 to 5, 90 in all
- disc_labels: int32 [24], P('dp'), may hold values from 0 to 1
- logit_gain: float32 [512], replicated, may hold values from 0.1 to 1.9
- adv_weight: float32 [1], replicated, may hold values from 0.5 to 1.5
- train_step: int32 [1], replicated, may hold values from 1000 to 19999
- ln1_gain: float32 [512], replicated, may hold values from 0.1 to 1.9
- ln1_bias: float32 [512], replicated, may hold values from -1.5 to 1.5
- spatial_qkv: bfloat16 [3, 512, 512], P(None, None, 'tensor'), may hold values from -0.25 to 0.25
- spatial_out: bfloat16 [512, 512], P('tensor'), may hold values from -0.75 to 0.75
- ln2_gain: float32 [512], replicated, may hold values from 0.1 to 1.9
- ln2_bias: float32 [512], replicated, may hold values from -1.5 to 1.5
- temporal_qkv: bfloat16 [3, 512, 512], P(None, None, 'tensor'), may hold values from -0.25 to 0.25
- temporal_out: bfloat16 [512, 512], P('tensor'), may hold values from -0.5 to 0.5
- ln3_gain: float32 [512], replicated, may hold values from 0.1 to 1.9
- ln3_bias: float32 [512], replicated, may hold values from -1.5 to 1.5
- mlp_in: bfloat16 [512, 2048], P(None, 'tensor'), may hold values from -0.25 to 0.25
- mlp_out: bfloat16 [2048, 512], P('tensor'), may hold values from -0.125 to 0.125
Outputs:
- gen_out: bfloat16 [24, 5, 256, 512], P('dp', None, 'tensor')
- gen_in_grad: bfloat16 [24, 5, 256, 512], P('dp', None, 'tensor')
- disc_out: bfloat16 [24, 5, 256, 512], P('dp', None, 'tensor')
- disc_in_grad: bfloat16 [24, 5, 256, 512], P('dp', None, 'tensor')
- ln1_gain_grad: float32 [512], P('dp')
- ln1_bias_grad: float32 [512], P('dp')
- spatial_qkv_grad: float32 [3, 512, 512], P(None, 'dp', 'tensor')
- spatial_out_grad: float32 [512, 512], P('tensor', 'dp')
- ln2_gain_grad: float32 [512], P('dp')
- ln2_bias_grad: float32 [512], P('dp')
- temporal_qkv_grad: float32 [3, 512, 512], P(None, 'dp', 'tensor')
- temporal_out_grad: float32 [512, 512], P('tensor', 'dp')
- ln3_gain_grad: float32 [512], P('dp')
- ln3_bias_grad: float32 [512], P('dp')
- mlp_in_grad: float32 [512, 2048], P('dp', 'tensor')
- mlp_out_grad: float32 [2048, 512], P('tensor', 'dp')
Inputs may be any that keep to these rules, and one draw needn't show every extreme that they name: `gen_aspect`: 0 lays a frame's patches on a square grid, 1 on a grid twice as wide, 2 on a grid half as wide; windows are 8 x 8 patches. `disc_aspect`: as gen_aspect. `gen_frames`: frames at or beyond a clip's count are padding; some clip has 5. `disc_frames`: as gen_frames.
All inputs are finite; a program needn't handle non-finite values. No bound on the sum of `gen_frames` or of `disc_frames` on one device may be relied on, other than what follows from the above.
Results may differ from a plain program's by a relative error of at most 0.025.
Values may be sent and summed in bfloat16 or wider, within the bound.
No kernel may reach another device: no remote copies, remote signals or barrier semaphores. Data moves between devices by JAX's collectives and lax.ppermute only.
A program may use at most 320 MiB of HBM per device.

v0:
```python
from functools import partial
import math

import jax
import jax.numpy as jnp
from jax import lax
from jax.experimental import pallas as pl
from jax.experimental.pallas import tpu as pltpu
from jax.sharding import PartitionSpec as P

HEAD_DIM = 64
WIN = 8
AREA = WIN * WIN
HALF = 5000
EPS = 1e-05
F32 = jnp.float32
BF16 = jnp.bfloat16
VMEM_LIMIT = 58 * 1024 * 1024
JOIN = 3
COEFS = tuple(math.sqrt(math.pi / 2.0) * a for a in (0.254829592, -0.284496736, 1.421413741, -1.453152027, 1.061405429))

NT = (((1,), (1,)), ((), ()))
TN = (((0,), (0,)), ((), ()))


def dot(lhs, rhs):
    return jnp.dot(lhs, rhs, preferred_element_type=F32)


def dot_nt(lhs, rhs):
    return lax.dot_general(lhs, rhs, NT, preferred_element_type=F32)


def dot_tn(lhs, rhs):
    return lax.dot_general(lhs, rhs, TN, preferred_element_type=F32)


def normalize(value):
    average = jnp.mean(value, axis=-1, keepdims=True)
    centred = value - average
    variance = jnp.mean(centred * centred, axis=-1, keepdims=True)
    scale = lax.rsqrt(variance + EPS)
    return centred * scale, scale


def norm_backward(unit, scale, gain, grad):
    scaled = grad * gain
    inner = scaled - jnp.mean(scaled, axis=-1, keepdims=True)
    return scale * (inner - unit * jnp.mean(scaled * unit, axis=-1, keepdims=True))


def row_sums(values):
    return jnp.sum(values.reshape(-1, 8, values.shape[-1]), axis=0)


ANY = pl.BlockSpec(memory_space=pl.ANY)
SMEM = pl.BlockSpec(memory_space=pltpu.SMEM)


def run(kernel, microseconds, grid, ins, in_specs, outs, out_specs, scratch=(), after=(), bases=()):
    ins, after, bases = tuple(ins), tuple(after), tuple(bases)
    count, extra = len(ins), len(after) + len(bases)

    def body(*refs):
        kernel(*refs[:count], *refs[count + extra :])

    return pl.pallas_call(
        body,
        grid=grid,
        in_specs=list(in_specs) + [ANY] * extra,
        out_specs=list(out_specs),
        out_shape=list(outs),
        scratch_shapes=list(scratch),
        input_output_aliases={count + len(after) + i: i for i in range(len(bases))},
        cost_estimate=pl.CostEstimate(flops=int(microseconds * 2.5e9), bytes_accessed=0, transcendentals=0),
        compiler_params=pltpu.CompilerParams(
            dimension_semantics=("arbitrary",) * len(grid), vmem_limit_bytes=VMEM_LIMIT
        ),
    )(*ins, *after, *bases)


def shape(dims, dtype=BF16):
    return jax.ShapeDtypeStruct(tuple(dims), dtype)


def whole(dims):
    zeros = (0,) * len(dims)
    return pl.BlockSpec(tuple(dims), lambda i: zeros)


def per_clip(dims, first=0, count=None):
    zeros = (0,) * (len(dims) - 1)
    count = count or dims[0]
    return pl.BlockSpec((1,) + tuple(dims[1:]), lambda i: (first + jnp.clip(i, 0, count - 1),) + zeros)


def join_rows(w_ref, part):
    return jnp.concatenate(
        [
            jnp.concatenate([part(w_ref, i, j) for j in range(w_ref.shape[1])], axis=1)
            for i in range(w_ref.shape[0])
        ],
        axis=0,
    )


def head_weight(w_ref, m):
    return join_rows(w_ref, lambda ref, i, j: ref[i, j, :, m * 128 : (m + 1) * 128])


def out_weight(w_ref):
    part = w_ref.shape[2] // 4
    return jnp.concatenate(
        [
            jnp.concatenate([w_ref[i, j, c * part : (c + 1) * part, 384:512] for c in range(4)], axis=1)
            for j in range(w_ref.shape[1])
            for i in range(w_ref.shape[0])
        ],
        axis=0,
    )


def hidden_weight(w_ref, j, n):
    part = w_ref.shape[2] // 2
    return jnp.concatenate([w_ref[i, j, n * part : (n + 1) * part, :] for i in range(w_ref.shape[0])], axis=0)


def head_mask(dtype):
    rows = lax.broadcasted_iota(jnp.int32, (256, 256), 0) // HEAD_DIM
    cols = lax.broadcasted_iota(jnp.int32, (256, 256), 1) // HEAD_DIM
    return jnp.where(rows == cols, 1.0, 0.0).astype(dtype)


def spread(values, mask):
    return jnp.concatenate([values] * 4, axis=0) * mask


def pair_product(scores, values, low_lane):
    parts = []
    for c in range(2):
        full = dot_tn(scores[:, c * 128 : (c + 1) * 128], values[:, c * 128 : (c + 1) * 128])
        parts.append(jnp.where(low_lane, full[:64], full[64:]))
    return jnp.concatenate(parts, axis=1)


def one_hot(source, count):
    rows = source.shape[0]
    inside = lax.broadcasted_iota(jnp.int32, (rows, count), 0) % 8
    cols = lax.broadcasted_iota(jnp.int32, (rows, count), 1)
    return jnp.where((source >= 0) & (cols == source * 8 + inside), 1.0, 0.0).astype(BF16)


def chunk_ids():
    return lax.broadcasted_iota(jnp.int32, (AREA, 1), 0) // 8


def send_source(aspect, t):
    c = chunk_ids()
    square = jnp.where(c < 4, 2 * c + 1 - t % 2, -1)
    wide = jnp.where(
        c < 2, 4 * c + (t ^ 1), jnp.where(c < 4, -1, jnp.where(c < 6, 4 * (c - 4) + (t ^ 2), 4 * (c - 6) + (t ^ 3)))
    )
    return jnp.where(aspect == 0, square, jnp.where(aspect == 1, wide, -1))


def window_source(aspect, t):
    c = chunk_ids()
    square = jnp.where(c < 4, 2 * c + t % 2, c + 4)
    wide = jnp.where(c < 2, 4 * c + t, jnp.where(c < 4, c + 10, jnp.where(c < 6, c + 4, c + 8)))
    return jnp.where(aspect == 0, square, jnp.where(aspect == 1, wide, c))


def raster_source(aspect, t):
    c = chunk_ids()
    square = c // 2 + jnp.where(c % 2 == t % 2, 0, 8)
    way = (c % 4) ^ t
    wide = c // 4 + jnp.where(way == 0, 0, jnp.where(way == 1, 8, jnp.where(way == 2, 12, 14)))
    return jnp.where(aspect == 0, square, jnp.where(aspect == 1, wide, c))


def write_sends(values, refs):
    if not refs:
        return
    for f in range(values.shape[0] // AREA):
        base = f * AREA
        refs[0][0, f * 32 : (f + 1) * 32, :] = values[base + 32 : base + 64]
        refs[1][0, f * 16 : (f + 1) * 16, :] = values[base + 16 : base + 32]
        refs[2][0, f * 16 : (f + 1) * 16, :] = values[base + 48 : base + 64]


def pack_rows(values, select, refs):
    for f in range(values.shape[0] // AREA):
        moved = dot(select, values[f * AREA : (f + 1) * AREA]).astype(BF16)
        refs[0][0, f * 32 : (f + 1) * 32, :] = moved[:32]
        refs[1][0, f * 16 : (f + 1) * 16, :] = moved[32:48]
        refs[2][0, f * 16 : (f + 1) * 16, :] = moved[48:]


def join_parts(source, own_ref, part_refs, out_ref):
    select = one_hot(source, 2 * AREA)
    for f in range(out_ref.shape[1] // AREA):
        rows = [own_ref[0, f * AREA : (f + 1) * AREA, :]]
        rows += [ref[0, f * size : (f + 1) * size, :] for ref, size in zip(part_refs, (32, 16, 16))]
        out_ref[0, f * AREA : (f + 1) * AREA, :] = dot(select, jnp.concatenate(rows, axis=0)).astype(BF16)


def pack_kernel(place_ref, aspect_ref, x_ref, *send_refs):
    select = one_hot(send_source(aspect_ref[pl.program_id(0)], place_ref[0]), AREA)
    pack_rows(x_ref[0], select, send_refs)


def pack_grad_kernel(place_ref, aspect_ref, count_ref, ramp_ref, rec_ref, adv_ref, dy_ref, *send_refs):
    clip = pl.program_id(0)
    frame = lax.broadcasted_iota(jnp.int32, (rec_ref.shape[1], 1), 0) // AREA
    total = rec_ref[0].astype(F32) + ramp_ref[0] * adv_ref[0].astype(F32)
    dy_ref[0] = jnp.where(frame < count_ref[clip], total, 0.0).astype(BF16)
    select = one_hot(send_source(aspect_ref[clip], place_ref[0]), AREA)
    pack_rows(dy_ref[0], select, send_refs)


def join_kernel(place_ref, aspect_ref, own_ref, *refs):
    i = pl.program_id(0)
    source = raster_source(aspect_ref[i], place_ref[0])
    passes = len(refs) // 4
    count = pl.num_programs(0) // passes
    for n in range(passes):

        @pl.when(i // count == n)
        def _():
            join_parts(source, own_ref, refs[3 * n : 3 * n + 3], refs[3 * passes + n])


def send_shapes(x):
    clips, rows, width = x.shape
    return [shape((clips, rows // part, width)) for part in (2, 4, 4)]


def head_spec(w, n):
    if w.shape[2] != 128:
        return whole(w.shape)
    return pl.BlockSpec(w.shape[:2] + (64, w.shape[3]), lambda i: (0, 0, n, 0))


def clip_specs(arrays, first=0, count=None):
    return [per_clip(a.shape, first, count) for a in arrays]


def whole_specs(arrays):
    return [whole(a.shape) for a in arrays]


def pack(place, aspect, x, after=()):
    outs = send_shapes(x)
    return run(
        pack_kernel, 0.01, x.shape[:1], (place, aspect, x), [SMEM, SMEM, per_clip(x.shape)], outs, clip_specs(outs), after=after
    )


def pack_grad(place, aspect, count, ramp, rec, adv, after=()):
    outs = [shape(rec.shape)] + send_shapes(rec)
    ins = (place, aspect, count, ramp, rec, adv)
    return run(
        pack_grad_kernel, 4, rec.shape[:1], ins, [SMEM] * 4 + clip_specs((rec, adv)), outs, clip_specs(outs), after=after
    )


def join_raster(place, aspect, own, parts, after=()):
    clips = parts[0][0].shape[0]

    def specs(arrays, n):
        return [pl.BlockSpec((1,) + a.shape[1:], lambda i: (jnp.clip(i - n * clips, 0, clips - 1), 0, 0)) for a in arrays]

    outs = [shape((clips,) + own.shape[1:])] * len(parts)
    ins = (place, aspect, own, *[p for group in parts for p in group])
    in_specs = [SMEM] * 2 + [per_clip(own.shape)] + [spec for n, group in enumerate(parts) for spec in specs(group, n)]
    out_specs = [spec for n, out in enumerate(outs) for spec in specs([out], n)]
    return run(join_kernel, JOIN * len(parts), own.shape[:1], ins, in_specs, outs, out_specs, after=after)


def exchange(parts):
    return tuple(swap(part, "tensor", way) for way, part in zip((1, 2, 3), parts))


def swap(x, axis, way):
    return lax.ppermute(x, axis, [(i, i ^ way) for i in range(lax.axis_size(axis))])


def place_products(place_ref, block_ref, out_refs, cols):
    for k in range(8):
        rows = pl.ds(pl.multiple_of((place_ref[1] ^ k) * 64, 64), 64)
        for j in range(4):
            lanes = pl.ds(pl.multiple_of((place_ref[0] ^ j) * 128, 128), 128)
            out_refs[k % 2][k // 2, j, 0:64, cols] = block_ref[rows, lanes].astype(BF16)


def attention_products(place_ref, a_ref, dqkv_ref, low_ref, o_ref, turned_ref, block_ref, out_refs):
    def flat(ref, cols=slice(None)):
        values = ref[:, :, cols]
        return values.reshape(-1, values.shape[-1])

    turned_ref[...] = flat(a_ref).T
    for m in range(3):
        block_ref[...] = dot(turned_ref[...], flat(dqkv_ref, slice(m * 512, (m + 1) * 512)))
        place_products(place_ref, block_ref, out_refs, slice(m * 128, (m + 1) * 128))
    turned_ref[...] = flat(low_ref).T
    block_ref[...] = dot(turned_ref[...], flat(o_ref))
    place_products(place_ref, block_ref, out_refs, slice(384, 512))


def product_scratch(clips, rows, width):
    return [
        pltpu.VMEM((clips, rows, 3 * width), BF16),
        *[pltpu.VMEM((clips, rows, width), BF16)] * 3,
        pltpu.VMEM((width, clips * rows), BF16),
        pltpu.VMEM((width, width), F32),
    ]


def window_blocks(rows):
    return [(w, g) for w in range(rows // AREA) for g in range(2)]


def low_lanes():
    return lax.broadcasted_iota(jnp.int32, (64, 128), 1) < HEAD_DIM


def space_forward_kernel(parts, place_ref, aspect_ref, x_ref, *refs):
    part_refs = refs[:parts]
    gain_ref, bias_ref, w_ref, x1_ref, qkv_ref, p_ref, o_ref, xw_ref, a_ref = refs[parts:]
    rows = x_ref.shape[1]
    if parts:
        join_parts(window_source(aspect_ref[pl.program_id(0)], place_ref[0]), x_ref, part_refs, xw_ref)
    else:
        xw_ref[...] = x_ref[...]
    x = xw_ref[0].astype(F32)
    unit, _ = normalize(x)
    a_ref[...] = (unit * gain_ref[...] + bias_ref[...]).astype(BF16)
    for j in range(3):
        qkv_ref[0, :, j * 512 : (j + 1) * 512] = dot(a_ref[...], head_weight(w_ref, j)).astype(BF16)
    mask, low_lane = head_mask(BF16), low_lanes()

    def part(j, w, g):
        return qkv_ref[0, w * AREA : (w + 1) * AREA, j * 512 + g * 256 : j * 512 + (g + 1) * 256]

    blocks = window_blocks(rows)
    scores = [dot_nt(part(1, w, g), spread(part(0, w, g), mask)) * 0.125 for w, g in blocks]
    for s, (w, g) in zip(scores, blocks):
        e = jnp.exp(s - jnp.max(s, axis=0, keepdims=True))
        p_ref[0, 2 * w + g] = (e * (1.0 / jnp.sum(e, axis=0, keepdims=True))).astype(BF16)
    for w, g in blocks:
        attended = pair_product(p_ref[0, 2 * w + g], part(2, w, g), low_lane)
        o_ref[0, w * AREA : (w + 1) * AREA, g * 256 : (g + 1) * 256] = attended.astype(BF16)
    x1_ref[0] = x + dot(o_ref[0], out_weight(w_ref))


def space_forward(place, aspect, x, parts, gain, bias, w, total, bases=(), after=()):
    clips, rows, width = x.shape
    first = total - clips if bases else 0
    outs = [
        shape((total, rows, width), F32),
        shape((total, rows, 3 * width)),
        shape((total, 2 * rows // AREA, AREA, 256)),
        shape((total, rows, width)),
        shape((total, rows, width)),
    ]
    return run(
        partial(space_forward_kernel, len(parts)), 10, (clips,), (place, aspect, x, *parts, gain, bias, w),
        [SMEM] * 2 + clip_specs((x, *parts)) + whole_specs((gain, bias)) + [head_spec(w, 0)], outs, clip_specs(outs, first, clips),
        [pltpu.VMEM((rows, width), BF16)], after, bases,
    )


def space_backward_clip(dx1, x, gain, bias, w_ref, qkv_ref, p_ref, dqkv_ref, low_ref, a_ref, do_ref):
    low_ref[...] = dx1.astype(BF16)
    do_ref[...] = dot_nt(low_ref[...], out_weight(w_ref)).astype(BF16)
    mask, low_lane = head_mask(BF16), low_lanes()

    def part(j, w, g):
        return qkv_ref[0, w * AREA : (w + 1) * AREA, j * 512 + g * 256 : j * 512 + (g + 1) * 256]

    def grad(w, g):
        return spread(do_ref[w * AREA : (w + 1) * AREA, g * 256 : (g + 1) * 256], mask)

    def put(j, w, g, values):
        dqkv_ref[w * AREA : (w + 1) * AREA, j * 512 + g * 256 : j * 512 + (g + 1) * 256] = values.astype(BF16)

    blocks = window_blocks(low_ref.shape[0])
    grad_probs = [dot_nt(part(2, w, g), grad(w, g)) for w, g in blocks]
    for w, g in blocks:
        put(2, w, g, dot(p_ref[0, 2 * w + g], grad(w, g)))
    grad_scores = []
    for dp, (w, g) in zip(grad_probs, blocks):
        p = p_ref[0, 2 * w + g].astype(F32)
        weighted = p * dp
        grad_scores.append((weighted - p * jnp.sum(weighted, axis=0, keepdims=True)).astype(BF16))
    for ds, (w, g) in zip(grad_scores, blocks):
        put(1, w, g, dot(ds, spread(part(0, w, g), mask)) * 0.125)
    for ds, (w, g) in zip(grad_scores, blocks):
        put(0, w, g, pair_product(ds, part(1, w, g), low_lane) * 0.125)
    da = dot_nt(dqkv_ref[...], jnp.concatenate([head_weight(w_ref, j) for j in range(3)], axis=1))
    unit, scale = normalize(x)
    a_ref[...] = (unit * gain + bias).astype(BF16)
    return dx1 + norm_backward(unit, scale, gain, da), row_sums(da * unit), row_sums(da)


def space_backward_kernel(
    dx1_ref, x_ref, gain_ref, bias_ref, w_ref, qkv_ref, p_ref, dqkv_ref, low_ref, a_ref, dx0_ref, dg_ref, db_ref, *rest
):
    *send_refs, do_ref = rest

    @pl.when(pl.program_id(0) == 0)
    def _():
        dg_ref[...] = jnp.zeros_like(dg_ref)
        db_ref[...] = jnp.zeros_like(db_ref)

    dx0, dg, db = space_backward_clip(
        dx1_ref[0], x_ref[0].astype(F32), gain_ref[...], bias_ref[...], w_ref, qkv_ref, p_ref,
        dqkv_ref.at[0], low_ref.at[0], a_ref.at[0], do_ref,
    )
    dx0_ref[0] = dx0.astype(BF16)
    write_sends(dx0_ref[0], send_refs)
    dg_ref[...] += dg
    db_ref[...] += db


def space_backward(direct, dx1, x, gain, bias, w, qkv, p, bases=(), after=()):
    total, rows, width = x.shape
    clips = total // 2
    first = clips if bases else 0
    kept = [shape((total, rows, 3 * width))] + [shape(x.shape)] * 2
    outs = [shape((clips, rows, width))]
    sums = [shape((8, width), F32)] * 2
    sends = send_shapes(outs[0]) if direct else []
    return run(
        space_backward_kernel, 10, (clips,), (dx1, x, gain, bias, w, qkv, p),
        clip_specs((dx1, x), first, clips) + whole_specs((gain, bias)) + [head_spec(w, 0)] + clip_specs((qkv, p), first, clips),
        kept + outs + sums + sends, clip_specs(kept, first, clips) + clip_specs(outs) + whole_specs(sums) + clip_specs(sends),
        [pltpu.VMEM((rows, width), BF16)], after, bases,
    )


def space_grad_kernel(place_ref, a_ref, dqkv_ref, low_ref, o_ref, *refs):
    norm_refs, (even_ref, odd_ref, turned_ref, block_ref) = refs[:-4], refs[-4:]
    i = pl.program_id(0)

    def place_block(m):
        place_products(place_ref, block_ref, (even_ref, odd_ref), slice(m * 128, (m + 1) * 128))

    @pl.when(i == 0)
    def _():
        turned_ref[...] = a_ref[...].T
        sums = [
            jnp.sum(left[...] + right[...], axis=0, keepdims=True) for left, right in zip(norm_refs[::2], norm_refs[1::2])
        ]
        sums = jnp.concatenate(sums + [jnp.zeros((16 - len(sums), 512), F32)], axis=0).astype(BF16)
        for ref in (even_ref, odd_ref):
            for k in range(4):
                for j in range(4):
                    ref[k, j, 64:80, :] = sums

    for m in range(3):

        @pl.when(i == m)
        def _():
            block_ref[...] = dot(turned_ref[...], dqkv_ref[...])
            place_block(m)

    @pl.when(i == 3)
    def _():
        turned_ref[...] = low_ref[...].T
        block_ref[...] = dot(turned_ref[...], o_ref[...])
        place_block(3)


def space_grad(place, a, dqkv, low, o, norms, after=()):
    a, dqkv, low, o = (v.reshape(-1, v.shape[-1]) for v in (a, dqkv, low, o))
    rows, width = a.shape
    outs = [shape((4, 4, 80, 512))] * 2
    column = pl.BlockSpec((rows, width), lambda i: (0, jnp.minimum(i, 2)))
    return run(
        space_grad_kernel, 6, (4,), (place, a, dqkv, low, o, *norms),
        [SMEM, whole(a.shape), column] + whole_specs((low, o, *norms)), outs, whole_specs(outs),
        [pltpu.VMEM((width, rows), BF16), pltpu.VMEM((width, width), F32)], after,
    )


def head_select(frame):
    rows = lax.broadcasted_iota(jnp.int32, (512, 128), 0) // HEAD_DIM
    cols = lax.broadcasted_iota(jnp.int32, (512, 128), 1) - 8 * frame
    return jnp.where(rows == cols, 1.0, 0.0).astype(BF16)


def head_expand(frame):
    rows = lax.broadcasted_iota(jnp.int32, (128, 512), 0) - 8 * frame
    cols = lax.broadcasted_iota(jnp.int32, (128, 512), 1) // HEAD_DIM
    return jnp.where(rows == cols, 1.0, 0.0).astype(BF16)


def head_sums(products, selector):
    high = products.astype(BF16)
    rest = (products - high.astype(F32)).astype(BF16)
    return dot(high, selector) + dot(rest, selector)


def time_scores(frames, left, right):
    totals = [None] * frames
    for t in range(frames):
        lhs = left(t).astype(F32)
        stacked = jnp.concatenate([lhs * right(f).astype(F32) for f in range(t + 1)], axis=0)
        sums = head_sums(stacked, head_select(t))
        for f in range(t + 1):
            part = sums[f * AREA : (f + 1) * AREA]
            totals[f] = part if totals[f] is None else totals[f] + part
    return totals


def time_forward_kernel(x_ref, gain_ref, bias_ref, w_ref, x2_ref, qkv_ref, p_ref, o_ref, a_ref):
    frames = x_ref.shape[1] // AREA
    x = x_ref[0]
    unit, _ = normalize(x)
    a_ref[...] = (unit * gain_ref[...] + bias_ref[...]).astype(BF16)
    for j in range(3):
        qkv_ref[0, :, j * 512 : (j + 1) * 512] = dot(a_ref[...], head_weight(w_ref, j)).astype(BF16)

    def part(j):
        return lambda f: qkv_ref[0, f * AREA : (f + 1) * AREA, j * 512 : (j + 1) * 512]

    scores = time_scores(frames, part(0), part(1))
    lane = lax.broadcasted_iota(jnp.int32, (AREA, 128), 1)
    scores = [jnp.where(lane >= 8 * f, s * 0.125, -1e30) for f, s in enumerate(scores)]
    top = scores[0]
    for s in scores[1:]:
        top = jnp.maximum(top, s)
    exps = [jnp.exp(s - top) for s in scores]
    inverse = 1.0 / sum(exps)
    probs = [e * inverse for e in exps]
    for f in range(frames):
        p_ref[0, f * AREA : (f + 1) * AREA, :] = probs[f]
    low = [p.astype(BF16) for p in probs]
    values = part(2)
    for t in range(frames):
        wide = dot(jnp.concatenate(low[: t + 1], axis=0), head_expand(t))
        total = None
        for f in range(t + 1):
            term = wide[f * AREA : (f + 1) * AREA] * values(f).astype(F32)
            total = term if total is None else total + term
        o_ref[0, t * AREA : (t + 1) * AREA, :] = total.astype(BF16)
    x2_ref[0] = x + dot(o_ref[0], out_weight(w_ref))


def time_forward(x, gain, bias, w, clips, bases=(), after=()):
    total, rows, width = x.shape
    first = total - clips if bases else 0
    outs = [
        shape((total, rows, width), F32),
        shape((total, rows, 3 * width)),
        shape((total, rows, 128), F32),
        shape((total, rows, width)),
    ]
    return run(
        time_forward_kernel, 10, (clips,), (x, gain, bias, w),
        clip_specs((x,), first, clips) + whole_specs((gain, bias)) + [head_spec(w, 1)],
        outs, clip_specs(outs, first, clips), [pltpu.VMEM((rows, width), BF16)], after, bases,
    )


def time_backward_clip(dx2, x, gain, bias, w_ref, qkv_ref, p_ref, dqkv_ref, low_ref, a_ref, do_ref):
    frames = low_ref.shape[0] // AREA
    low_ref[...] = dx2.astype(BF16)
    do_ref[...] = dot_nt(low_ref[...], out_weight(w_ref)).astype(BF16)

    def part(j):
        return lambda f: qkv_ref[0, f * AREA : (f + 1) * AREA, j * 512 : (j + 1) * 512]

    queries, key_rows, values = part(0), part(1), part(2)

    def grads(t):
        return do_ref[t * AREA : (t + 1) * AREA, :]

    dp = time_scores(frames, grads, values)
    probs = [p_ref[0, f * AREA : (f + 1) * AREA, :] for f in range(frames)]
    inner = sum(p * d for p, d in zip(probs, dp))
    ds = [(p * (d - inner)).astype(BF16) for p, d in zip(probs, dp)]
    low = [p.astype(BF16) for p in probs]
    dk = [None] * frames
    dv = [None] * frames
    for t in range(frames):
        wide = dot(jnp.concatenate(ds[: t + 1] + low[: t + 1], axis=0), head_expand(t))
        q, do = queries(t).astype(F32), grads(t).astype(F32)
        dq = None
        for f in range(t + 1):
            ds_wide = wide[f * AREA : (f + 1) * AREA]
            p_wide = wide[(t + 1 + f) * AREA : (t + 2 + f) * AREA]
            term = ds_wide * key_rows(f).astype(F32)
            dq = term if dq is None else dq + term
            dk[f] = ds_wide * q if dk[f] is None else dk[f] + ds_wide * q
            dv[f] = p_wide * do if dv[f] is None else dv[f] + p_wide * do
        dqkv_ref[t * AREA : (t + 1) * AREA, 0:512] = (dq * 0.125).astype(BF16)
    for f in range(frames):
        dqkv_ref[f * AREA : (f + 1) * AREA, 512:1024] = (dk[f] * 0.125).astype(BF16)
        dqkv_ref[f * AREA : (f + 1) * AREA, 1024:1536] = dv[f].astype(BF16)
    da = dot_nt(dqkv_ref[...], jnp.concatenate([head_weight(w_ref, j) for j in range(3)], axis=1))
    unit, scale = normalize(x)
    a_ref[...] = (unit * gain + bias).astype(BF16)
    return dx2 + norm_backward(unit, scale, gain, da), row_sums(da * unit), row_sums(da)


def time_backward_kernel(
    place_ref, dx2_ref, x_ref, gain_ref, bias_ref, w_ref, qkv_ref, p_ref, o_ref, dx1_ref, dg_ref, db_ref, *refs
):
    *out_refs, do_ref, dqkv_all, low_all, a_all, o_all, turned_ref, block_ref = refs
    i, count = pl.program_id(0), dqkv_all.shape[0]

    @pl.when(i == 0)
    def _():
        dg_ref[...] = jnp.zeros_like(dg_ref)
        db_ref[...] = jnp.zeros_like(db_ref)

    @pl.when(i < count)
    def _():
        o_all[i] = o_ref[0]
        dx1, dg, db = time_backward_clip(
            dx2_ref[0], x_ref[0], gain_ref[...], bias_ref[...], w_ref, qkv_ref, p_ref,
            dqkv_all.at[i], low_all.at[i], a_all.at[i], do_ref,
        )
        dx1_ref[0] = dx1
        dg_ref[...] += dg
        db_ref[...] += db

    @pl.when(i == count)
    def _():
        attention_products(place_ref, a_all, dqkv_all, low_all, o_all, turned_ref, block_ref, out_refs)


def time_backward(place, dx2, x, gain, bias, w, qkv, p, o, after=()):
    clips, rows, width = x.shape
    sums = [shape((8, width), F32)] * 2 + [shape((4, 4, 64, 512))] * 2
    ins = (place, dx2, x, gain, bias, w, qkv, p, o)
    return run(
        time_backward_kernel, 26, (clips + 1,), ins,
        [SMEM] + clip_specs((dx2, x)) + whole_specs((gain, bias)) + [head_spec(w, 1)] + clip_specs((qkv, p, o)),
        [shape(x.shape, F32)] + sums, [per_clip(x.shape)] + whole_specs(sums),
        [pltpu.VMEM((rows, width), BF16)] + product_scratch(clips, rows, width), after,
    )


def gelu_parts(h):
    e = jnp.exp2(h * h * (-0.5 * math.log2(math.e)) + math.log2(1.0 / math.sqrt(2.0 * math.pi)))
    t = pl.reciprocal(1.0 + (0.3275911 * math.sqrt(0.5)) * jnp.abs(h), approx=True)
    tail = t * (COEFS[0] + t * (COEFS[1] + t * (COEFS[2] + t * (COEFS[3] + t * COEFS[4])))) * e
    cdf = jnp.where(h >= 0, 1.0 - tail, tail)
    return h * cdf, cdf + h * e


def mlp_clip(x, gain, bias, w_ref, c_ref, gb_ref, u_ref, dh_ref, slope_ref, y_ref, send_refs, grad_of):
    tiles = w_ref.shape[1]
    unit, scale = normalize(x)
    c_ref[...] = (unit * gain + bias).astype(BF16)
    for j in range(tiles):
        active, slope = gelu_parts(dot(c_ref[...], hidden_weight(w_ref, j, 0)))
        u_ref[j] = active.astype(BF16)
        slope_ref[j] = slope.astype(BF16)
    y = x + dot(
        jnp.concatenate([u_ref[j] for j in range(tiles)], axis=1),
        jnp.concatenate([hidden_weight(w_ref, j, 1) for j in range(tiles)], axis=0),
    )
    y_ref[...] = y.astype(BF16)
    write_sends(y_ref[...], send_refs)
    dy = grad_of(y)
    for j in range(tiles):
        du = dot_nt(gb_ref[...], hidden_weight(w_ref, j, 1))
        dh_ref[j] = (du * slope_ref[j].astype(F32)).astype(BF16)
    dc = dot_nt(
        jnp.concatenate([dh_ref[j] for j in range(tiles)], axis=1),
        jnp.concatenate([hidden_weight(w_ref, j, 0) for j in range(tiles)], axis=1),
    )
    return dy + norm_backward(unit, scale, gain, dc), row_sums(dc * unit), row_sums(dc)


def mlp_gen_kernel(parts, place_ref, aspect_ref, x_ref, gain_ref, bias_ref, w_ref, grad_ref, *rest):
    part_refs = rest[:parts]
    y_ref, dx_ref, c_ref, gb_ref, u_ref, dh_ref, dg_ref, db_ref, *send_refs, slope_ref = rest[parts:]
    i = pl.program_id(0)

    @pl.when(i == 0)
    def _():
        dg_ref[...] = jnp.zeros_like(dg_ref)
        db_ref[...] = jnp.zeros_like(db_ref)

    if parts:
        join_parts(window_source(aspect_ref[i], place_ref[0]), grad_ref, part_refs, gb_ref)
    else:
        gb_ref[...] = grad_ref[...]
    dx, dg, db = mlp_clip(
        x_ref[0], gain_ref[...], bias_ref[...], w_ref, c_ref.at[0], gb_ref.at[0], u_ref.at[:, 0], dh_ref.at[:, 0], slope_ref,
        y_ref.at[0], send_refs, lambda y: gb_ref[0].astype(F32),
    )
    dx_ref[0] = dx
    dg_ref[...] += dg
    db_ref[...] += db


def tile_block(dims, count):
    return pl.BlockSpec((dims[0], 1) + tuple(dims[2:]), lambda i: (0, jnp.minimum(i, count - 1), 0, 0))


def mlp_gen(direct, place, aspect, x, gain, bias, w, grad, parts=(), after=()):
    total, rows, width = x.shape
    clips, tiles, span = total // 2, w.shape[1], w.shape[3]
    both = [shape(x.shape), shape(x.shape, F32)]
    kept = [shape((clips, rows, width))] * 2
    hidden = [shape((tiles, clips, rows, span))] * 2
    sums = [shape((8, width), F32)] * 2
    sends = send_shapes(kept[0]) if direct else []
    return run(
        partial(mlp_gen_kernel, len(parts)), 20, (clips,), (place, aspect, x, gain, bias, w, grad, *parts),
        [SMEM] * 2 + clip_specs((x,), 0, clips) + whole_specs((gain, bias, w)) + clip_specs((grad, *parts)),
        both + kept + hidden + sums + sends,
        clip_specs(both, 0, clips) + clip_specs(kept) + [tile_block(h.shape, clips) for h in hidden] + whole_specs(sums) + clip_specs(sends),
        [pltpu.VMEM((tiles, rows, span), BF16)], after,
    )


def mlp_disc_kernel(
    sign_ref, count_ref, place_ref, x_ref, gain_ref, bias_ref, w_ref, logit_ref, c_gen, gb_gen, u_gen, dh_gen, dg_gen, db_gen,
    y_ref, dx_ref, out_ref, dg_ref, db_ref, *rest,
):
    send_refs, (slope_ref, c_all, gb_all, u_all, dh_all, turned_ref, block_ref) = rest[:-7], rest[-7:]
    i, (tiles, total, rows, span) = pl.program_id(0), u_all.shape
    count = total // 2

    @pl.when(i == 0)
    def _():
        dg_ref[...] = dg_gen[...]
        db_ref[...] = db_gen[...]

    @pl.when(i < count)
    def _():
        at = count + i
        c_all[i] = c_gen[0]
        gb_all[i] = gb_gen[0]
        u_all[:, i] = u_gen[:, 0]
        dh_all[:, i] = dh_gen[:, 0]

        def grad_of(y):
            sign = sign_ref[i]
            frame = lax.broadcasted_iota(jnp.int32, (rows, 1), 0) // AREA
            live = jnp.where(frame < count_ref[i], -sign, 0.0)
            dy = live * logit_ref[...] * jax.nn.sigmoid(1.0 - sign * logit_ref[...] * y)
            gb_all[at] = dy.astype(BF16)
            return dy

        dx, dg, db = mlp_clip(
            x_ref[0], gain_ref[...], bias_ref[...], w_ref, c_all.at[at], gb_all.at[at], u_all.at[:, at], dh_all.at[:, at],
            slope_ref, y_ref.at[0], send_refs, grad_of,
        )
        dx_ref[0] = dx
        dg_ref[...] += dg
        db_ref[...] += db

    @pl.when(i == count)
    def _():
        turned_ref[0] = c_all[...].reshape(-1, c_all.shape[2]).T
        turned_ref[1] = gb_all[...].reshape(-1, gb_all.shape[2]).T

    @pl.when(i >= count)
    def _():
        at = place_ref[0] ^ (i - count)
        for n, right in enumerate((dh_all, u_all)):
            block_ref[...] = dot(turned_ref[n], right[at].reshape(-1, span))
            for k in range(8):
                out_ref[k, 0, n * 64 : (n + 1) * 64, :] = block_ref[k * 64 : (k + 1) * 64, :].astype(BF16)


def mlp_disc(direct, sign, count, place, x, gain, bias, w, logit, kept, hidden, sums, bases, after=()):
    total, rows, width = x.shape
    clips, tiles, span = total // 2, w.shape[1], w.shape[3]
    outs = [shape(x.shape), shape(x.shape, F32)]
    blocks = shape((8, tiles, 128, span))
    sends = send_shapes(kept[0]) if direct else []
    ins = (sign, count, place, x, gain, bias, w, logit, *kept, *hidden, *sums)
    return run(
        mlp_disc_kernel, 30, (clips + tiles,), ins,
        [SMEM] * 3 + clip_specs((x,), clips, clips) + whole_specs((gain, bias, w, logit)) + clip_specs(kept)
        + [tile_block(h.shape, clips) for h in hidden] + whole_specs(sums),
        outs + [blocks] + [shape(v.shape, F32) for v in sums] + sends,
        clip_specs(outs, clips, clips) + [pl.BlockSpec((8, 1, 128, span), lambda i: (0, jnp.clip(i - clips, 0, tiles - 1), 0, 0))]
        + whole_specs(sums) + clip_specs(sends),
        [
            pltpu.VMEM((tiles, rows, span), BF16),
            pltpu.VMEM((total, rows, width), BF16),
            pltpu.VMEM((total, rows, width), BF16),
            pltpu.VMEM((tiles, total, rows, span), BF16),
            pltpu.VMEM((tiles, total, rows, span), BF16),
            pltpu.VMEM((2, width, total * rows), BF16),
            pltpu.VMEM((width, span), F32),
        ],
        after, bases,
    )


def window_maps(aspect, tokens_frame):
    grid_side = math.isqrt(tokens_frame)
    grid_width = jnp.where(
        aspect == 1, 2 * grid_side, jnp.where(aspect == 2, grid_side // 2, grid_side)
    ).astype(jnp.int32)[:, None]
    across = grid_width // WIN
    places = jnp.arange(tokens_frame, dtype=jnp.int32)[None, :]
    window = places // AREA
    inside = places % AREA
    grid_row = window // across * WIN + inside // WIN
    grid_col = window % across * WIN + inside % WIN
    forward_order = grid_row * grid_width + grid_col
    raster_row = places // grid_width
    raster_col = places % grid_width
    back_order = (
        (raster_row // WIN * across + raster_col // WIN) * AREA + raster_row % WIN * WIN + raster_col % WIN
    )
    return (forward_order, back_order)


def reorder(values, order):
    return jax.vmap(partial(jnp.take, axis=1))(values, order)


def pad_clips(values, split):
    return jnp.pad(values, [(0, -values.shape[0] % split)] + [(0, 0)] * (values.ndim - 1))


def gather_window(x, aspect, split):
    whole_x = pad_clips(lax.all_gather(x, "tensor", axis=2, tiled=True), split)
    aspect = pad_clips(aspect, split)
    t = lax.axis_index("tensor")
    clips = aspect.shape[0] // split
    mine = lax.dynamic_slice_in_dim(whole_x, t % split * clips, clips, 0)
    kinds = lax.dynamic_slice_in_dim(aspect, t % split * clips, clips, 0)
    order, _ = window_maps(kinds, whole_x.shape[2])
    return reorder(mine, lax.dynamic_slice_in_dim(order, t // split * AREA, AREA, 1))


def gather_raster(y, aspect, split, patches):
    every = lax.all_gather(y, "tensor", axis=0)
    count, clips, frames, _, width = every.shape
    every = every.reshape(count // split, split, clips, frames, AREA, width)
    every = jnp.transpose(every, (1, 2, 3, 0, 4, 5)).reshape(split * clips, frames, -1, width)
    _, back = window_maps(aspect, every.shape[2])
    t = lax.axis_index("tensor")
    return reorder(every[: aspect.shape[0]], lax.dynamic_slice_in_dim(back, t * patches, patches, 1))


def attention_piece(d, w_ref, wo_ref):
    rows = w_ref.shape[1] // 8
    part = wo_ref.shape[0] // 8
    qkv = [w_ref[m, pl.ds(pl.multiple_of(d * rows, rows), rows), :] for m in range(3)]
    out = wo_ref[pl.ds(pl.multiple_of(d * part, part), part), :]
    squares = [out[:, c * 128 : (c + 1) * 128] for c in range(out.shape[1] // 128)]
    return jnp.concatenate(qkv + [jnp.concatenate(squares, axis=0)], axis=1)


def pack_weights_kernel(place_ref, sw_ref, swo_ref, tw_ref, two_ref, w_in_ref, w_out_ref, heads_ref, hidden_ref):
    d = place_ref[1]
    heads_ref[0:64, :] = attention_piece(d, sw_ref, swo_ref)
    heads_ref[64:128, :] = attention_piece(d, tw_ref, two_ref)
    rows = pl.ds(pl.multiple_of(d * 64, 64), 64)
    hidden_ref[0:64, :] = w_in_ref[rows, :]
    hidden_ref[64:128, :] = w_out_ref[rows, :]


def pack_weights(place, *weights):
    outs = [shape((128, 512))] * 2
    return run(pack_weights_kernel, 0.01, (1,), (place, *weights), [SMEM] + whole_specs(weights), outs, whole_specs(outs))


def stack_kernel(place_ref, *refs):
    for j in range(4):
        refs[4][place_ref[0] ^ j] = refs[j][...]


def stack_pieces(place, pieces, after=()):
    outs = [shape((4,) + pieces[0].shape)]
    ins = (place, *pieces)
    return run(stack_kernel, 0.01, (1,), ins, [SMEM] + whole_specs(pieces), outs, whole_specs(outs), after=after)[0]


def gather_shard(shard):
    rows = shard.shape[0] // lax.axis_size("dp")
    piece = lax.dynamic_slice_in_dim(shard, lax.axis_index("dp") * rows, rows, 0)
    whole_w = lax.all_gather(piece, ("tensor", "dp"), axis=0, tiled=True)
    return whole_w.reshape((-1,) + shard.shape)


def gather_attention(w, wo):
    width = wo.shape[1]
    heads = gather_shard(w.reshape(-1, w.shape[2])).reshape((-1,) + w.shape)
    heads = jnp.moveaxis(heads, 0, 2).reshape(3, width, 4, -1).transpose(2, 1, 0, 3).reshape(4, width, -1)
    out = gather_shard(wo).reshape(4, width // 4, 4, width // 4).transpose(0, 2, 1, 3).reshape(4, width, -1)
    return jnp.concatenate([heads, out], axis=2)[None]


def gather_hidden(w_in, w_out):
    columns = jnp.moveaxis(gather_shard(w_in), 0, 1).reshape(w_in.shape[0], 4, -1)
    rows = gather_shard(w_out).reshape(4, -1, w_out.shape[1])
    return jnp.concatenate([jnp.moveaxis(columns, 1, 0), rows], axis=1)[None]


def add_kernel(count, *refs):
    operands, outs = refs[:count], refs[count:]
    for i, out in enumerate(outs):
        total = operands[0][i].astype(F32)
        for operand in operands[1:]:
            total = total + operand[i].astype(F32)
        out[...] = total.astype(out.dtype)


def add_blocks(operands, dtype=BF16, after=()):
    outs = [shape(operands[0].shape[1:], dtype)] * operands[0].shape[0]
    return run(
        partial(add_kernel, len(operands)), 0.01, (1,), operands, whole_specs(operands), outs, whole_specs(outs), after=after
    )


def reduce_core(even, odd, after=()):
    return add_blocks([even, swap(odd, "dp", 1)], after=after)


def chips_kernel(*refs):
    ins, out_refs = refs[:8], refs[8:]
    for j, out in enumerate(out_refs):
        at = 0
        for group in (ins[:4], ins[4:]):
            rows = group[0].shape[1]
            out[at : at + rows] = sum(ref[j].astype(F32) for ref in group).astype(BF16)
            at += rows


def chip_parts(near):
    return [near[0]] + [swap(near[i], "dp", 2 * i) for i in (1, 2, 3)]


def reduce_chips(ours, others, after=()):
    outs = [shape((ours[0].shape[1] + others[0].shape[1], ours[0].shape[2]))] * 4
    ins = (*ours, *others)
    return run(chips_kernel, 0.01, (1,), ins, whole_specs(ins), outs, whole_specs(outs), after=after)


def reduce_tensor(mine, after=()):
    parts = [mine[0]] + [swap(mine[j], "tensor", j) for j in (1, 2, 3)]
    return add_blocks([p[None] for p in parts], F32, after)[0]


def scatter_grad(grads):
    flat = jnp.concatenate([g.astype(BF16).reshape(g.shape[0], -1) for g in grads], axis=1)
    flat = lax.psum_scatter(flat, "dp", scatter_dimension=0, tiled=True)
    pieces, offset = [], 0
    count = lax.axis_size("tensor")
    for g in grads:
        size = math.prod(g.shape[1:])
        piece = flat[:, offset : offset + size].reshape((flat.shape[0],) + g.shape[1:])
        pieces.append(jnp.moveaxis(piece, 2, 0).reshape(count, flat.shape[0], -1))
        offset += size
    mine = lax.psum_scatter(jnp.concatenate(pieces, axis=2), "tensor", scatter_dimension=0, tiled=True)[0]
    results, offset = [], 0
    for g in grads:
        size = g.shape[1] * g.shape[3]
        results.append(mine[:, offset : offset + size].reshape(-1, g.shape[1], g.shape[3]).astype(F32))
        offset += size
    return results


def in_order(even, odd):
    blocks = jnp.stack([even[:, :, :64], odd[:, :, :64]], axis=1).reshape(8, 4, 64, 4, 128)
    return jnp.transpose(blocks, (0, 2, 3, 1, 4)).reshape(512, 4, 512)


def shards(
    gen_tokens, rec_grad, adv_grad, gen_aspect, gen_frames, disc_tokens, disc_aspect, disc_frames, disc_labels,
    logit_gain, adv_weight, train_step, ln1_gain, ln1_bias, spatial_qkv, spatial_out, ln2_gain, ln2_bias,
    temporal_qkv, temporal_out, ln3_gain, ln3_bias, mlp_in, mlp_out,
):
    tensor = lax.axis_size("tensor")
    dp_at, tensor_at = lax.axis_index("dp"), lax.axis_index("tensor")
    local, frames, patches, width = gen_tokens.shape
    windows = patches * tensor // AREA
    direct = tensor == 4 and windows == 4 and lax.axis_size("dp") == 8
    split = max(tensor // windows, 1)
    clips = -(-local // split)
    place = jnp.stack([tensor_at, dp_at]).astype(jnp.int32)
    vectors = [v.reshape(1, -1) for v in (ln1_gain, ln1_bias, ln2_gain, ln2_bias, ln3_gain, ln3_bias, logit_gain)]
    g1, b1, g2, b2, g3, b3, logit = vectors

    step_value = train_step.astype(F32)
    ramp = adv_weight * step_value / (step_value + HALF)

    def mine(values):
        return lax.dynamic_slice_in_dim(pad_clips(values, split), tensor_at % split * clips, clips, 0)

    count = mine(disc_frames)
    sign = (2 * mine(disc_labels) - 1).astype(F32)
    aspects = (mine(gen_aspect), mine(disc_aspect))

    def flat(x):
        return x.reshape(x.shape[0], -1, width)

    if direct:
        x_gen, x_disc, rec, adv = (flat(v) for v in (gen_tokens, disc_tokens, rec_grad, adv_grad))
        heads, hidden = pack_weights(place, spatial_qkv, spatial_out, temporal_qkv, temporal_out, mlp_in, mlp_out)
        gen_parts = pack(place, gen_aspect, x_gen, (heads,))
        disc_parts = pack(place, disc_aspect, x_disc, gen_parts)
        dy, *dy_parts = pack_grad(place, gen_aspect, gen_frames, ramp, rec, adv, disc_parts)
        heads = [heads] + [swap(heads, "tensor", j) for j in (1, 2, 3)]
        heads = stack_pieces(place, heads, (dy,))
        space_w = time_w = lax.all_gather(heads, "dp", axis=0)
        gen_parts = exchange(gen_parts)
        hidden = [hidden] + [swap(hidden, "tensor", j) for j in (1, 2, 3)]
        hidden = stack_pieces(place, hidden, (heads, *gen_parts))
        mlp_w = lax.all_gather(hidden, "dp", axis=0)
        disc_parts, dy_parts = exchange(disc_parts), exchange(dy_parts)
    else:
        place = jnp.zeros_like(place)
        space_w, time_w = gather_attention(spatial_qkv, spatial_out), gather_attention(temporal_qkv, temporal_out)
        mlp_w = gather_hidden(mlp_in, mlp_out)
        x_gen = flat(gather_window(gen_tokens, gen_aspect, split))
        x_disc = flat(gather_window(disc_tokens, disc_aspect, split))
        live = jnp.arange(frames, dtype=jnp.int32)[None, :] < gen_frames[:, None]
        total = rec_grad.astype(F32) + ramp[0] * adv_grad.astype(F32)
        dy = jnp.where(live[:, :, None, None], total, 0.0).astype(BF16)
        dy = flat(gather_window(dy, gen_aspect, split))
        gen_parts, disc_parts, dy_parts = (), (), ()

    sf = space_forward(place, aspects[0], x_gen, gen_parts, g1, b1, space_w, 2 * clips, (), (hidden,) if direct else ())
    tf = time_forward(sf[0], g2, b2, time_w, clips)
    sf = space_forward(place, aspects[1], x_disc, disc_parts, g1, b1, space_w, 2 * clips, sf, tf[:1])
    x1, s_qkv, s_p, s_o, xw = sf
    x2, t_qkv, t_p, t_o = time_forward(x1, g2, b2, time_w, clips, tf)
    gen = mlp_gen(direct, place, aspects[0], x2, g3, b3, mlp_w, dy, dy_parts)
    y_gen = exchange(gen[8:]) if direct else ()
    y, dx2, ff_blocks, ff_dg, ff_db, *y_sends = mlp_disc(
        direct, sign, count, place, x2, g3, b3, mlp_w, logit, gen[2:4], gen[4:6], gen[6:8], gen[:2]
    )
    y_disc = exchange(y_sends) if direct else ()
    if direct:
        ff_mine = lax.psum_scatter(ff_blocks, "dp", scatter_dimension=0)
    dx1, t_dg, t_db, t_even, t_odd = time_backward(place, dx2, x1, g2, b2, time_w, t_qkv, t_p, t_o, y_gen)
    back = space_backward(direct, dx1, xw, g1, b1, space_w, s_qkv, s_p, (), y_disc)
    kept, (dx0_gen, s_dg, s_db, *gen_sends) = back[:3], back[3:]
    if direct:
        t_near = reduce_core(t_even, t_odd, (dx0_gen,))
        gen_parts = exchange(gen_sends)
        t_parts = chip_parts(t_near)
    back = space_backward(
        direct, dx1, xw, g1, b1, space_w, s_qkv, s_p, kept, (t_near[0],) if direct else ()
    )
    kept, (dx0_disc, d_dg, d_db, *disc_sends) = back[:3], back[3:]
    disc_parts = exchange(disc_sends) if direct else ()
    dqkv, low, a = kept
    zero = jnp.zeros_like(t_dg)
    s_even, s_odd = space_grad(
        place, a, dqkv, low, s_o, (s_dg, d_dg, s_db, d_db, t_dg, zero, t_db, zero, ff_dg, zero, ff_db, zero),
        (dx0_disc, ff_mine, *t_parts) if direct else (),
    )

    part = width // tensor
    if direct:
        ff_share = reduce_tensor(ff_mine)
        both = jnp.concatenate([gen_aspect, disc_aspect])
        outs = join_raster(place, both, y, (y_gen, y_disc), (s_even, ff_share))
        near = reduce_core(s_even, s_odd, (*gen_parts, *outs))
        dx_gen = join_raster(place, gen_aspect, dx0_gen, (gen_parts,), near[:1])
        ours = reduce_chips(chip_parts(near), t_parts, dx_gen)
        dx_disc = join_raster(place, disc_aspect, dx0_disc, (disc_parts,), ours[:1])
        share = reduce_tensor(ours)
        small = share[64:70]
        in_share, out_share = ff_share[:64], ff_share[64:]
        shares = []
        for block in (share[:64], share[80:]):
            shares += [jnp.moveaxis(block[:, : 3 * part].reshape(-1, 3, part), 1, 0), block[:, 3 * part :].T]
        y_gen, y_disc, dx_gen, dx_disc = (v.reshape(gen_tokens.shape) for v in (*outs, *dx_gen, *dx_disc))
    else:
        y_gen, y_disc, dx_gen, dx_disc = (
            gather_raster(v.reshape(clips, frames, AREA, width), aspect, split, patches)
            for v, aspect in ((y[:clips], gen_aspect), (y[clips:], disc_aspect), (dx0_gen, gen_aspect), (dx0_disc, disc_aspect))
        )
        ff = jnp.transpose(ff_blocks.reshape(8, 4, 2, 64, 512), (0, 3, 2, 1, 4)).reshape(width, 2, tensor, -1)
        ff_share = scatter_grad([ff])[0]
        in_share, out_share = ff_share[:, 0], ff_share[:, 1]
        shares = []
        for even, odd in ((s_even, s_odd), (t_even, t_odd)):
            block = scatter_grad([in_order(even, odd).reshape(width, 4, tensor, part)])[0]
            shares += [jnp.moveaxis(block[:, :3], 1, 0), block[:, 3].T]
        small = lax.psum(s_even[0, 0, 64:70].astype(F32), ("dp", "tensor"))
    piece = width // lax.axis_size("dp")
    small = lax.dynamic_slice_in_dim(small, dp_at * piece, piece, 1)

    return (
        y_gen, dx_gen, y_disc, dx_disc,
        small[0], small[1], shares[0], shares[1], small[2], small[3], shares[2], shares[3],
        small[4], small[5], in_share, out_share.T,
    )


def solution(mesh):
    tokens = P("dp", None, "tensor", None)
    vector, clip = P(), P("dp")
    qkv, rows, cols = P(None, None, "tensor"), P("tensor", None), P(None, "tensor")
    in_specs = (
        (tokens,) * 3 + (clip,) * 2 + (tokens,) + (clip,) * 3 + (vector,) * 5
        + (qkv, rows, vector, vector, qkv, rows, vector, vector, cols, rows)
    )
    block = (clip, clip, P(None, "dp", "tensor"), P("tensor", "dp"))
    out_specs = (tokens,) * 4 + block * 2 + (clip, clip, P("dp", "tensor"), P("tensor", "dp"))
    return jax.shard_map(shards, mesh=mesh, in_specs=in_specs, out_specs=out_specs, check_vma=False)
```

profile of v0, /device:TPU:0, one launch (start us, length us, event | category | flops | bytes accessed | tf_op | source)
XLA Modules:
  0.0 326.3 jit_solution(8245704849372581975)
XLA Ops:
  10.1 3.0 collective-permute-start.3
  17.0 3.3 %shard_map.352 = (bf16[3,160,512]{2,1,0:T(8,128)(2,1)}, bf16[3,80,512]{2,1,0:T(8,128)(2,1)}, bf16[3,80,512]{2,1,0:T(8,128)(2,1)}) custom-call(s32[2]{0:T(128)} %pad_add_fusion.refs_0_.refs_2_, s32[3]{0:T(128)} %refs_1_.14, bf16[3,320,512]{2,1,0:T(8,128)(2,1)} %bitcast.61, bf16[128,512]{1,0:T(8,128)(2,1)} %get-tuple-element.104.refs_3_.refs_1_), custom_call_target="tpu_custom_call" | custom-call | flops 25000000 | tf_op jit(solution)/shard_map/pallas_call | solution.py:67
  20.4 3.3 %shard_map.353 = (bf16[3,160,512]{2,1,0:T(8,128)(2,1)}, bf16[3,80,512]{2,1,0:T(8,128)(2,1)}, bf16[3,80,512]{2,1,0:T(8,128)(2,1)}) custom-call(s32[2]{0:T(128)} %pad_add_fusion.refs_0_.refs_2_, s32[3]{0:T(128)} %refs_1_.15, bf16[3,320,512]{2,1,0:T(8,128)(2,1)} %bitcast.59, bf16[3,160,512]{2,1,0:T(8,128)(2,1)} %get-tuple-element.105.refs_3_, ...), custom_call_target="tpu_custom_call" | custom-call | flops 25000000 | tf_op jit(solution)/shard_map/pallas_call | solution.py:67
  23.7 4.0 %shard_map.354 = (bf16[3,320,512]{2,1,0:T(8,128)(2,1)}, bf16[3,160,512]{2,1,0:T(8,128)(2,1)}, bf16[3,80,512]{2,1,0:T(8,128)(2,1)}, bf16[3,80,512]{2,1,0:T(8,128)(2,1)}) custom-call(s32[2]{0:T(128)} %pad_add_fusion.refs_0_.refs_2_, s32[3]{0:T(128)} %refs_1_.14, s32[3]{0:T(128)} %refs_2_.3, f32[1]{0:T(128)S(6)} %div.3.refs_3_, bf16[3,320,512]{2,1,0:T(8,128)(2,1)} %bitcast.85, ...), custom_call_target="tpu_custom_call" | custom-call | flops 10000000000 | tf_op jit(solution)/shard_map/pallas_call | solution.py:67
  31.5 3.5 %collective-permute-start.10 = (bf16[128,512]{1,0:T(8,128)(2,1)S(1)}, bf16[128,512]{1,0:T(8,128)(2,1)S(1)}, u32[]{:S(2)}, u32[]{:S(2)}) collective-permute-start(bf16[128,512]{1,0:T(8,128)(2,1)S(1)} %copy-done.21), channel_id=1, source_target_pairs={{0,2},{1,3},{2,0},{3,1},{4,6},{5,7},{6,4},{7,5},{8,10},{9,11},{10,... | collective-permute-start | bytes 393224 | tf_op jit(solution)/shard_map/ppermute | solution.py:285
  38.9 7.2 %collective-permute-done.10.refs_3_ = bf16[128,512]{1,0:T(8,128)(2,1)S(1)} collective-permute-done((bf16[128,512]{1,0:T(8,128)(2,1)S(1)}, bf16[128,512]{1,0:T(8,128)(2,1)S(1)}, u32[]{:S(2)}, u32[]{:S(2)}) %collective-permute-start.10) | collective-permute-done | bytes 131104 | tf_op jit(solution)/shard_map/ppermute | solution.py:285
  46.0 4.0 %collective-permute-start.9 = (bf16[128,512]{1,0:T(8,128)(2,1)S(1)}, bf16[128,512]{1,0:T(8,128)(2,1)S(1)}, u32[]{:S(2)}, u32[]{:S(2)}) collective-permute-start(bf16[128,512]{1,0:T(8,128)(2,1)S(1)} %copy-done.21), channel_id=1, source_target_pairs={{0,1},{1,0},{2,3},{3,2},{4,5},{5,4},{6,7},{7,6},{8,9},{9,8},{10,11... | collective-permute-start | bytes 393224 | tf_op jit(solution)/shard_map/ppermute | solution.py:285
  51.1 11.3 %collective-permute-done.11.refs_4_ = bf16[128,512]{1,0:T(8,128)(2,1)S(1)} collective-permute-done((bf16[128,512]{1,0:T(8,128)(2,1)S(1)}, bf16[128,512]{1,0:T(8,128)(2,1)S(1)}, u32[]{:S(2)}, u32[]{:S(2)}) %collective-permute-start.11) | collective-permute-done | bytes 131104 | tf_op jit(solution)/shard_map/ppermute | solution.py:285
  62.5 5.6 %collective-permute-start = (bf16[3,160,512]{2,1,0:T(8,128)(2,1)S(1)}, bf16[3,160,512]{2,1,0:T(8,128)(2,1)S(1)}, u32[]{:S(2)}, u32[]{:S(2)}) collective-permute-start(bf16[3,160,512]{2,1,0:T(8,128)(2,1)S(1)} %copy-done.36), channel_id=1, source_target_pairs={{0,1},{1,0},{2,3},{3,2},{4,5},{5,4},{6,7},{7,6},{8,9},{9,8},{10,11... | collective-permute-start | bytes 1474568 | tf_op jit(solution)/shard_map/ppermute | solution.py:285
  75.1 9.3 %shard_map.357 = (f32[6,320,512]{2,1,0:T(8,128)}, bf16[6,320,1536]{2,1,0:T(8,128)(2,1)}, bf16[6,10,64,256]{3,2,1,0:T(8,128)(2,1)}, bf16[6,320,512]{2,1,0:T(8,128)(2,1)}, bf16[6,320,512]{2,1,0:T(8,128)(2,1)}) custom-call(s32[2]{0:T(128)} %pad_add_fusion.refs_0_.refs_2_, s32[3]{0:T(128)} %refs_1_.14, bf16[3,320,512]{2,1,0:T(8,128)(2,1)} %bitcast.62, ...), custom_call_target="tpu_custom_call" | custom-call | flops 24999999488 | tf_op jit(solution)/shard_map/pallas_call | solution.py:67
  84.4 10.2 %shard_map.358 = (f32[6,320,512]{2,1,0:T(8,128)}, bf16[6,320,1536]{2,1,0:T(8,128)(2,1)}, f32[6,320,128]{2,1,0:T(8,128)}, bf16[6,320,512]{2,1,0:T(8,128)(2,1)}) custom-call(f32[6,320,512]{2,1,0:T(8,128)} %get-tuple-element.113.refs_0_.refs_10_, f32[1,512]{1,0:T(1,128)} %bitcast.92, f32[1,512]{1,0:T(1,128)} %bitcast.95, bf16[8,4,128,512]{3,2,1,0:T(8,128)(2,1)} %bitcast.77), custom_call_target="tpu_custom_call" | custom-call | flops 24999999488 | tf_op jit(solution)/shard_map/pallas_call | solution.py:67
  97.6 8.9 %shard_map.359 = (f32[6,320,512]{2,1,0:T(8,128)}, bf16[6,320,1536]{2,1,0:T(8,128)(2,1)}, bf16[6,10,64,256]{3,2,1,0:T(8,128)(2,1)}, bf16[6,320,512]{2,1,0:T(8,128)(2,1)}, bf16[6,320,512]{2,1,0:T(8,128)(2,1)}) custom-call(s32[2]{0:T(128)} %pad_add_fusion.refs_0_.refs_2_, ...), custom_call_target="tpu_custom_call", output_to_operand_aliasing={{0}: (10, {}), {1}: (11, {}), {2}: (12, {}), {3}: (13, {}),... | custom-call | flops 24999999488 | tf_op jit(solution)/shard_map/pallas_call | solution.py:67
  106.5 10.5 %shard_map.360 = (f32[6,320,512]{2,1,0:T(8,128)}, bf16[6,320,1536]{2,1,0:T(8,128)(2,1)}, f32[6,320,128]{2,1,0:T(8,128)}, bf16[6,320,512]{2,1,0:T(8,128)(2,1)}) custom-call(f32[6,320,512]{2,1,0:T(8,128)} %get-tuple-element.119.refs_0_.refs_2_, f32[1,512]{1,0:T(1,128)} %bitcast.93, ...), custom_call_target="tpu_custom_call", output_to_operand_aliasing={{0}: (4, {}), {1}: (5, {}), {2}: (6, {}), {3}: (7, {})} | custom-call | flops 24999999488 | tf_op jit(solution)/shard_map/pallas_call | solution.py:67
  118.1 19.5 %shard_map.361 = (bf16[6,320,512]{2,1,0:T(8,128)(2,1)}, f32[6,320,512]{2,1,0:T(8,128)}, bf16[3,320,512]{2,1,0:T(8,128)(2,1)}, bf16[3,320,512]{2,1,0:T(8,128)(2,1...) custom-call(s32[2]{0:T(128)} %pad_add_fusion.refs_0_.refs_2_, ...), custom_call_target="tpu_custom_call" | custom-call | flops 49999998976 | tf_op jit(solution)/shard_map/pallas_call | solution.py:67
  142.1 31.8 %shard_map.362 = (bf16[6,320,512]{2,1,0:T(8,128)(2,1)}, f32[6,320,512]{2,1,0:T(8,128)}, bf16[8,4,128,512]{3,2,1,0:T(8,128)(2,1)}, f32[8,512]{1,0:T(8,128)}, f32[...) custom-call(f32[3]{0:T(128)} %add_convert_fusion.refs_0_, ...), custom_call_target="tpu_custom_call", output_to_operand_aliasing={{0}: (14, {}), {1}: (15, {})} | custom-call | flops 74999996416 | tf_op jit(solution)/shard_map/pallas_call | solution.py:67
  180.3 27.2 %shard_map.363 = (f32[6,320,512]{2,1,0:T(8,128)}, f32[8,512]{1,0:T(8,128)}, f32[8,512]{1,0:T(8,128)}, bf16[4,4,64,512]{3,2,1,0:T(8,128)(2,1)}, bf16[4,4,64,512]{3,2,1,0:T(8,128)(2,1)}) custom-call(s32[2]{0:T(128)} %pad_add_fusion.refs_0_.refs_2_, f32[6,320,512]{2,1,0:T(8,128)} %get-tuple-element.142.refs_1_, ...), custom_call_target="tpu_custom_call" | custom-call | flops 65000001536 | tf_op jit(solution)/shard_map/pallas_call | solution.py:67
  208.5 10.1 %shard_map.364 = (bf16[6,320,1536]{2,1,0:T(8,128)(2,1)}, bf16[6,320,512]{2,1,0:T(8,128)(2,1)}, bf16[6,320,512]{2,1,0:T(8,128)(2,1)}, bf16[3,320,512]{2,1,0:T(8,1...) custom-call(f32[6,320,512]{2,1,0:T(8,128)} %get-tuple-element.146.re, ...), custom_call_target="tpu_custom_call" | custom-call | flops 24999999488 | tf_op jit(solution)/shard_map/pallas_call | solution.py:67
  228.5 10.3 %shard_map.366 = (bf16[6,320,1536]{2,1,0:T(8,128)(2,1)}, bf16[6,320,512]{2,1,0:T(8,128)(2,1)}, bf16[6,320,512]{2,1,0:T(8,128)(2,1)}, bf16[3,320,512]{2,1,0:T(8,1...) custom-call(f32[6,320,512]{2,1,0:T(8,128)} %get-tuple-element.146.re, ...), custom_call_target="tpu_custom_call", output_to_operand_aliasing={{0}: (8, {}), {1}: (9, {}), {2}: (10, {})} | custom-call | flops 24999999488 | tf_op jit(solution)/shard_map/pallas_call | solution.py:67
  245.6 11.6 %shard_map.367 = (bf16[4,4,80,512]{3,2,1,0:T(8,128)(2,1)}, bf16[4,4,80,512]{3,2,1,0:T(8,128)(2,1)}) custom-call(s32[2]{0:T(128)} %pad_add_fusion.refs_0_.refs_2_, bf16[1920,512]{1,0:T(8,128)(2,1)} %bitcast.108, bf16[1920,1536]{1,0:T(8,128)(2,1)} %bitcast.106, bf16[1920,512]{1,0:T(8,128)(2,1)} %bitcast.107, bf16[1920,512]{1,0:T(8,128)(2,1)} %bitcast.109, ...), custom_call_target="tpu_custom_call" | custom-call | flops 15000000512 | tf_op jit(solution)/shard_map/pallas_call | solution.py:67
  261.6 5.9 %shard_map.369 = (bf16[3,320,512]{2,1,0:T(8,128)(2,1)}, bf16[3,320,512]{2,1,0:T(8,128)(2,1)}) custom-call(s32[2]{0:T(128)} %pad_add_fusion.refs_0_.refs_2_, s32[6]{0:T(128)} %pad_add_fusion.1.refs_1_, bf16[6,320,512]{2,1,0:T(8,128)(2,1)} %get-tuple-element.135.refs_2_, bf16[3,160,512]{2,1,0:T(8,128)(2,1)} %copy-done.33, bf16[3,80,512]{2,1,0:T(8,128)(2,1)} %copy-done.41, ...), custom_call_target="tpu_custom_call" | custom-call | flops 15000000512 | tf_op jit(solution)/shard_map/pallas_call | solution.py:67
  284.6 3.7 %shard_map.371.refs_8_ = bf16[3,320,512]{2,1,0:T(8,128)(2,1)} custom-call(s32[2]{0:T(128)} %pad_add_fusion.refs_0_.refs_2_, s32[3]{0:T(128)} %refs_1_.14, bf16[3,320,512]{2,1,0:T(8,128)(2,1)} %get-tuple-element.152.refs_2_, bf16[3,160,512]{2,1,0:T(8,128)(2,1)} %copy-done.5, bf16[3,80,512]{2,1,0:T(8,128)(2,1)} %copy-done.12, bf16[3,80,512]{2,1,0:T(8,128)(2,1)} %copy-done.13, ...), custom_call_target="tpu_custom_call" | custom-call | flops 7500000256 | tf_op jit(solution)/shard_map/pallas_call | solution.py:67
  288.4 6.2 %collective-permute-done.36.refs_2_ = bf16[4,80,512]{2,1,0:T(8,128)(2,1)S(1)} collective-permute-done((bf16[4,80,512]{2,1,0:T(8,128)(2,1)}, bf16[4,80,512]{2,1,0:T(8,128)(2,1)S(1)}, u32[]{:S(2)}, u32[]{:S(2)}) %collective-permute-start.36) | collective-permute-done | bytes 327712 | tf_op jit(solution)/shard_map/ppermute | solution.py:285
  303.8 3.7 %shard_map.373 = bf16[3,320,512]{2,1,0:T(8,128)(2,1)} custom-call(s32[2]{0:T(128)} %pad_add_fusion.refs_0_.refs_2_, s32[3]{0:T(128)} %refs_1_.15, bf16[3,320,512]{2,1,0:T(8,128)(2,1)} %get-tuple-element.169.refs_17_.refs_2_, bf16[3,160,512]{2,1,0:T(8,128)(2,1)} %copy-done.39, bf16[3,80,512]{2,1,0:T(8,128)(2,1)} %copy-done.53, ...), custom_call_target="tpu_custom_call" | custom-call | flops 7500000256 | tf_op jit(solution)/shard_map/pallas_call | solution.py:67
  307.6 4.2 %collective-permute-done.39 = bf16[144,512]{1,0:T(8,128)(2,1)S(1)} collective-permute-done((bf16[144,512]{1,0:T(8,128)(2,1)}, bf16[144,512]{1,0:T(8,128)(2,1)S(1)}, u32[]{:S(2)}, u32[]{:S(2)}) %collective-permute-start.39) | collective-permute-done | bytes 147488 | tf_op jit(solution)/shard_map/ppermute | solution.py:285
  (226 shorter events, 91.8 us)
Async XLA Ops:
  7.2 67.9 %all-gather.5.cloned.1.call-start = ((), (), s32[]{:S(2)}) async-start(), calls=%async_computation.2 | async-start | bytes 4718592 | tf_op jit(solution)/shard_map/all_gather | solution.py:1012
  30.4 86.7 %all-gather.7.cloned.1.call-start = ((), (), s32[]{:S(2)}) async-start(), calls=%async_computation.3 | async-start | bytes 4718592 | tf_op jit(solution)/shard_map/all_gather | solution.py:1016
  30.5 41.1 %collective-permute-start.6 = (bf16[3,160,512]{2,1,0:T(8,128)(2,1)S(1)}, bf16[3,160,512]{2,1,0:T(8,128)(2,1)S(1)}, u32[]{:S(2)}, u32[]{:S(2)}) collective-permute-start(bf16[3,160,512]{2,1,0:T(8,128)(2,1)S(1)} %copy-done.3), channel_id=1, source_target_pairs={{0,1},{1,0},{2,3},{3,2},{4,5},{5,4},{6,7},{7,6},{8,9},{9,8},{10,11... | collective-permute-start | bytes 1474568 | tf_op jit(solution)/shard_map/ppermute | solution.py:285
  35.0 33.6 %collective-permute-start.7 = (bf16[3,80,512]{2,1,0:T(8,128)(2,1)S(1)}, bf16[3,80,512]{2,1,0:T(8,128)(2,1)S(1)}, u32[]{:S(2)}, u32[]{:S(2)}) collective-permute-start(bf16[3,80,512]{2,1,0:T(8,128)(2,1)S(1)} %copy-done.15), channel_id=1, source_target_pairs={{0,2},{1,3},{2,0},{3,1},{4,6},{5,7},{6,4},{7,5},{8,10},{9,11},{10,... | collective-permute-start | bytes 737288 | tf_op jit(solution)/shard_map/ppermute | solution.py:285
  35.0 35.5 %collective-permute-start.8 = (bf16[3,80,512]{2,1,0:T(8,128)(2,1)S(1)}, bf16[3,80,512]{2,1,0:T(8,128)(2,1)S(1)}, u32[]{:S(2)}, u32[]{:S(2)}) collective-permute-start(bf16[3,80,512]{2,1,0:T(8,128)(2,1)S(1)} %copy-done.14), channel_id=1, source_target_pairs={{0,3},{1,2},{2,1},{3,0},{4,7},{5,6},{6,5},{7,4},{8,11},{9,10},{10,... | collective-permute-start | bytes 737288 | tf_op jit(solution)/shard_map/ppermute | solution.py:285
  37.4 25.0 %collective-permute-start.11 = (bf16[128,512]{1,0:T(8,128)(2,1)S(1)}, bf16[128,512]{1,0:T(8,128)(2,1)S(1)}, u32[]{:S(2)}, u32[]{:S(2)}) collective-permute-start(bf16[128,512]{1,0:T(8,128)(2,1)S(1)} %copy-done.21), channel_id=1, source_target_pairs={{0,3},{1,2},{2,1},{3,0},{4,7},{5,6},{6,5},{7,4},{8,11},{9,10},{10,... | collective-permute-start | bytes 393224 | tf_op jit(solution)/shard_map/ppermute | solution.py:285
  62.5 34.3 %collective-permute-start = (bf16[3,160,512]{2,1,0:T(8,128)(2,1)S(1)}, bf16[3,160,512]{2,1,0:T(8,128)(2,1)S(1)}, u32[]{:S(2)}, u32[]{:S(2)}) collective-permute-start(bf16[3,160,512]{2,1,0:T(8,128)(2,1)S(1)} %copy-done.36), channel_id=1, source_target_pairs={{0,1},{1,0},{2,3},{3,2},{4,5},{5,4},{6,7},{7,6},{8,9},{9,8},{10,11... | collective-permute-start | bytes 1474568 | tf_op jit(solution)/shard_map/ppermute | solution.py:285
  68.0 26.6 %collective-permute-start.1 = (bf16[3,80,512]{2,1,0:T(8,128)(2,1)S(1)}, bf16[3,80,512]{2,1,0:T(8,128)(2,1)S(1)}, u32[]{:S(2)}, u32[]{:S(2)}) collective-permute-start(bf16[3,80,512]{2,1,0:T(8,128)(2,1)S(1)} %copy-done.50), channel_id=1, source_target_pairs={{0,2},{1,3},{2,0},{3,1},{4,6},{5,7},{6,4},{7,5},{8,10},{9,11},{10,... | collective-permute-start | bytes 737288 | tf_op jit(solution)/shard_map/ppermute | solution.py:285
  68.6 28.2 %collective-permute-start.2 = (bf16[3,80,512]{2,1,0:T(8,128)(2,1)S(1)}, bf16[3,80,512]{2,1,0:T(8,128)(2,1)S(1)}, u32[]{:S(2)}, u32[]{:S(2)}) collective-permute-start(bf16[3,80,512]{2,1,0:T(8,128)(2,1)S(1)} %copy-done.49), channel_id=1, source_target_pairs={{0,3},{1,2},{2,1},{3,0},{4,7},{5,6},{6,5},{7,4},{8,11},{9,10},{10,... | collective-permute-start | bytes 737288 | tf_op jit(solution)/shard_map/ppermute | solution.py:285
  70.5 46.6 %collective-permute-start.12 = (bf16[3,160,512]{2,1,0:T(8,128)(2,1)}, bf16[3,160,512]{2,1,0:T(8,128)(2,1)S(1)}, u32[]{:S(2)}, u32[]{:S(2)}) collective-permute-start(bf16[3,160,512]{2,1,0:T(8,128)(2,1)} %get-tuple-element.124), channel_id=1, source_target_pairs={{0,1},{1,0},{2,3},{3,2},{4,5},{5,4},{6,7},{7,6},{8,9},{9,8},{10,11... | collective-permute-start | bytes 1474568 | tf_op jit(solution)/shard_map/ppermute | solution.py:285
  71.6 45.4 %collective-permute-start.13 = (bf16[3,80,512]{2,1,0:T(8,128)(2,1)}, bf16[3,80,512]{2,1,0:T(8,128)(2,1)S(1)}, u32[]{:S(2)}, u32[]{:S(2)}) collective-permute-start(bf16[3,80,512]{2,1,0:T(8,128)(2,1)} %get-tuple-element.125), channel_id=1, source_target_pairs={{0,2},{1,3},{2,0},{3,1},{4,6},{5,7},{6,4},{7,5},{8,10},{9,11},{10,... | collective-permute-start | bytes 737288 | tf_op jit(solution)/shard_map/ppermute | solution.py:285
  75.0 163.8 %reduce-scatter.2.cloned.1.call-start = ((), (), s32[]{:S(2)}) async-start(), calls=%async_computation.1 | async-start | bytes 4718592 | tf_op jit(solution)/shard_map/reduce_scatter | solution.py:1042
  94.7 22.4 %collective-permute-start.14 = (bf16[3,80,512]{2,1,0:T(8,128)(2,1)S(1)}, bf16[3,80,512]{2,1,0:T(8,128)(2,1)S(1)}, u32[]{:S(2)}, u32[]{:S(2)}) collective-permute-start(bf16[3,80,512]{2,1,0:T(8,128)(2,1)S(1)} %copy-done.47), channel_id=1, source_target_pairs={{0,3},{1,2},{2,1},{3,0},{4,7},{5,6},{6,5},{7,4},{8,11},{9,10},{10,... | collective-permute-start | bytes 737288 | tf_op jit(solution)/shard_map/ppermute | solution.py:285
  137.6 41.8 %collective-permute-start.15 = (bf16[3,160,512]{2,1,0:T(8,128)(2,1)}, bf16[3,160,512]{2,1,0:T(8,128)(2,1)S(1)}, u32[]{:S(2)}, u32[]{:S(2)}) collective-permute-start(bf16[3,160,512]{2,1,0:T(8,128)(2,1)} %get-tuple-element.136), channel_id=1, source_target_pairs={{0,1},{1,0},{2,3},{3,2},{4,5},{5,4},{6,7},{7,6},{8,9},{9,8},{10,11... | collective-permute-start | bytes 1474568 | tf_op jit(solution)/shard_map/ppermute | solution.py:285
  138.3 39.6 %collective-permute-start.16 = (bf16[3,80,512]{2,1,0:T(8,128)(2,1)}, bf16[3,80,512]{2,1,0:T(8,128)(2,1)S(1)}, u32[]{:S(2)}, u32[]{:S(2)}) collective-permute-start(bf16[3,80,512]{2,1,0:T(8,128)(2,1)} %get-tuple-element.137), channel_id=1, source_target_pairs={{0,2},{1,3},{2,0},{3,1},{4,6},{5,7},{6,4},{7,5},{8,10},{9,11},{10,... | collective-permute-start | bytes 737288 | tf_op jit(solution)/shard_map/ppermute | solution.py:285
  140.6 38.8 %collective-permute-start.17 = (bf16[3,80,512]{2,1,0:T(8,128)(2,1)}, bf16[3,80,512]{2,1,0:T(8,128)(2,1)S(1)}, u32[]{:S(2)}, u32[]{:S(2)}) collective-permute-start(bf16[3,80,512]{2,1,0:T(8,128)(2,1)} %get-tuple-element.138), channel_id=1, source_target_pairs={{0,3},{1,2},{2,1},{3,0},{4,7},{5,6},{6,5},{7,4},{8,11},{9,10},{10,... | collective-permute-start | bytes 737288 | tf_op jit(solution)/shard_map/ppermute | solution.py:285
  174.9 32.7 %collective-permute-start.18 = (bf16[3,160,512]{2,1,0:T(8,128)(2,1)S(1)}, bf16[3,160,512]{2,1,0:T(8,128)(2,1)S(1)}, u32[]{:S(2)}, u32[]{:S(2)}) collective-permute-start(bf16[3,160,512]{2,1,0:T(8,128)(2,1)S(1)} %copy-done.40), channel_id=1, source_target_pairs={{0,1},{1,0},{2,3},{3,2},{4,5},{5,4},{6,7},{7,6},{8,9},{9,8},{10,11... | collective-permute-start | bytes 1474568 | tf_op jit(solution)/shard_map/ppermute | solution.py:285
  175.0 32.6 %collective-permute-start.19 = (bf16[3,80,512]{2,1,0:T(8,128)(2,1)S(1)}, bf16[3,80,512]{2,1,0:T(8,128)(2,1)S(1)}, u32[]{:S(2)}, u32[]{:S(2)}) collective-permute-start(bf16[3,80,512]{2,1,0:T(8,128)(2,1)S(1)} %copy-done.57), channel_id=1, source_target_pairs={{0,2},{1,3},{2,0},{3,1},{4,6},{5,7},{6,4},{7,5},{8,10},{9,11},{10,... | collective-permute-start | bytes 737288 | tf_op jit(solution)/shard_map/ppermute | solution.py:285
  177.9 29.7 %collective-permute-start.20 = (bf16[3,80,512]{2,1,0:T(8,128)(2,1)S(1)}, bf16[3,80,512]{2,1,0:T(8,128)(2,1)S(1)}, u32[]{:S(2)}, u32[]{:S(2)}) collective-permute-start(bf16[3,80,512]{2,1,0:T(8,128)(2,1)S(1)} %copy-done.56), channel_id=1, source_target_pairs={{0,3},{1,2},{2,1},{3,0},{4,7},{5,6},{6,5},{7,4},{8,11},{9,10},{10,... | collective-permute-start | bytes 737288 | tf_op jit(solution)/shard_map/ppermute | solution.py:285
  218.7 48.9 %collective-permute-start.28 = (bf16[3,160,512]{2,1,0:T(8,128)(2,1)}, bf16[3,160,512]{2,1,0:T(8,128)(2,1)S(1)}, u32[]{:S(2)}, u32[]{:S(2)}) collective-permute-start(bf16[3,160,512]{2,1,0:T(8,128)(2,1)} %get-tuple-element.176), channel_id=1, source_target_pairs={{0,1},{1,0},{2,3},{3,2},{4,5},{5,4},{6,7},{7,6},{8,9},{9,8},{10,11... | collective-permute-start | bytes 1474568 | tf_op jit(solution)/shard_map/ppermute | solution.py:285
  218.7 48.8 %collective-permute-start.29 = (bf16[3,80,512]{2,1,0:T(8,128)(2,1)}, bf16[3,80,512]{2,1,0:T(8,128)(2,1)S(1)}, u32[]{:S(2)}, u32[]{:S(2)}) collective-permute-start(bf16[3,80,512]{2,1,0:T(8,128)(2,1)} %get-tuple-element.177), channel_id=1, source_target_pairs={{0,2},{1,3},{2,0},{3,1},{4,6},{5,7},{6,4},{7,5},{8,10},{9,11},{10,... | collective-permute-start | bytes 737288 | tf_op jit(solution)/shard_map/ppermute | solution.py:285
  273.2 29.7 %collective-permute-start.32 = (bf16[3,160,512]{2,1,0:T(8,128)(2,1)S(1)}, bf16[3,160,512]{2,1,0:T(8,128)(2,1)S(1)}, u32[]{:S(2)}, u32[]{:S(2)}) collective-permute-start(bf16[3,160,512]{2,1,0:T(8,128)(2,1)S(1)} %copy-done.34), channel_id=1, source_target_pairs={{0,1},{1,0},{2,3},{3,2},{4,5},{5,4},{6,7},{7,6},{8,9},{9,8},{10,11... | collective-permute-start | bytes 1474568 | tf_op jit(solution)/shard_map/ppermute | solution.py:285
  273.7 27.5 %collective-permute-start.33 = (bf16[3,80,512]{2,1,0:T(8,128)(2,1)S(1)}, bf16[3,80,512]{2,1,0:T(8,128)(2,1)S(1)}, u32[]{:S(2)}, u32[]{:S(2)}) collective-permute-start(bf16[3,80,512]{2,1,0:T(8,128)(2,1)S(1)} %copy-done.44), channel_id=1, source_target_pairs={{0,2},{1,3},{2,0},{3,1},{4,6},{5,7},{6,4},{7,5},{8,10},{9,11},{10,... | collective-permute-start | bytes 737288 | tf_op jit(solution)/shard_map/ppermute | solution.py:285
  275.9 27.0 %collective-permute-start.34 = (bf16[3,80,512]{2,1,0:T(8,128)(2,1)S(1)}, bf16[3,80,512]{2,1,0:T(8,128)(2,1)S(1)}, u32[]{:S(2)}, u32[]{:S(2)}) collective-permute-start(bf16[3,80,512]{2,1,0:T(8,128)(2,1)S(1)} %copy-done.43), channel_id=1, source_target_pairs={{0,3},{1,2},{2,1},{3,0},{4,7},{5,6},{6,5},{7,4},{8,11},{9,10},{10,... | collective-permute-start | bytes 737288 | tf_op jit(solution)/shard_map/ppermute | solution.py:285
  (80 other events, 686.8 us)
Sparse Core Ops, SparseCore 0:
  30.6 38.1 all-gather.4
  75.1 36.2 all-gather.6
  174.1 51.3 reduce-scatter.1
where the time goes:
time: 330 us; the launch traced here: 326 us
  Pallas kernels  191 us (58%)
  starting transfers between devices  66.5 us (20%)
  waiting for transfers between devices  31.2 us (9%)
  local copies, waits for them, and re-layouts  19.5 us (6%)
  between operations  16 us (5%)
    pallas_call x24, Pallas kernels, run(): pl.pallas_call(body, grid=grid, in_specs=list(in_specs) + [ANY] * extra,...  191 us
    ppermute x41, starting transfers between devices, swap(): lax.ppermute(x, axis, [(i, i ^ way) for i in range(lax.axis_size(axis))])  66.4 us
    ppermute x41, waiting for transfers between devices, swap(): lax.ppermute(x, axis, [(i, i ^ way) for i in range(lax.axis_size(axis))])  31.1 us
    unnamed x122, local copies, waits for them, and re-layouts  12.6 us
  transfers between devices with their start and end apart: 44, of which 5 were waited for; matrix products, arithmetic and copies ran while one was open for 1% of the time, Pallas kernels for 50%

commit v1 on v0

--- a/solution.py
+++ b/solution.py
@@ -16,7 +16,7 @@
 F32 = jnp.float32
 BF16 = jnp.bfloat16
 VMEM_LIMIT = 58 * 1024 * 1024
-JOIN = 3
+JOIN = 0.01
 COEFS = tuple(math.sqrt(math.pi / 2.0) * a for a in (0.254829592, -0.284496736, 1.421413741, -1.453152027, 1.061405429))
 
 NT = (((1,), (1,)), ((), ()))
@@ -218,16 +218,9 @@
     pack_rows(dy_ref[0], select, send_refs)
 
 
-def join_kernel(place_ref, aspect_ref, own_ref, *refs):
-    i = pl.program_id(0)
-    source = raster_source(aspect_ref[i], place_ref[0])
-    passes = len(refs) // 4
-    count = pl.num_programs(0) // passes
-    for n in range(passes):
-
-        @pl.when(i // count == n)
-        def _():
-            join_parts(source, own_ref, refs[3 * n : 3 * n + 3], refs[3 * passes + n])
+def join_kernel(place_ref, aspect_ref, own_ref, r1_ref, r2_ref, r3_ref, out_ref):
+    source = raster_source(aspect_ref[pl.program_id(0)], place_ref[0])
+    join_parts(source, own_ref, (r1_ref, r2_ref, r3_ref), out_ref)
 
 
 def send_shapes(x):
@@ -264,17 +257,12 @@
     )
 
 
-def join_raster(place, aspect, own, parts, after=()):
+def join_raster(place, aspect, own, parts, first, microseconds, after=()):
     clips = parts[0][0].shape[0]
-
-    def specs(arrays, n):
-        return [pl.BlockSpec((1,) + a.shape[1:], lambda i: (jnp.clip(i - n * clips, 0, clips - 1), 0, 0)) for a in arrays]
-
-    outs = [shape((clips,) + own.shape[1:])] * len(parts)
-    ins = (place, aspect, own, *[p for group in parts for p in group])
-    in_specs = [SMEM] * 2 + [per_clip(own.shape)] + [spec for n, group in enumerate(parts) for spec in specs(group, n)]
-    out_specs = [spec for n, out in enumerate(outs) for spec in specs([out], n)]
-    return run(join_kernel, JOIN * len(parts), own.shape[:1], ins, in_specs, outs, out_specs, after=after)
+    outs = [shape((clips,) + own.shape[1:])]
+    ins = (place, aspect, own, *parts[0])
+    in_specs = [SMEM] * 2 + clip_specs((own,), first, clips) + clip_specs(parts[0])
+    return run(join_kernel, microseconds, (clips,), ins, in_specs, outs, clip_specs(outs), after=after)
 
 
 def exchange(parts):
@@ -765,7 +753,7 @@
 
     @pl.when(i >= count)
     def _():
-        at = place_ref[0] ^ (i - count)
+        at = i - count
         for n, right in enumerate((dh_all, u_all)):
             block_ref[...] = dot(turned_ref[n], right[at].reshape(-1, span))
             for k in range(8):
@@ -943,9 +931,28 @@
     return run(chips_kernel, 0.01, (1,), ins, whole_specs(ins), outs, whole_specs(outs), after=after)
 
 
-def reduce_tensor(mine, after=()):
-    parts = [mine[0]] + [swap(mine[j], "tensor", j) for j in (1, 2, 3)]
-    return add_blocks([p[None] for p in parts], F32, after)[0]
+def finish_kernel(place_ref, *refs):
+    parts, (s_qkv, s_out, t_qkv, t_out, *norms) = refs[:4], refs[4:-1]
+    sums_ref = refs[-1]
+    total = sum(part[...].astype(F32) for part in parts)
+    for block, qkv_ref, out_ref in ((total[0:64], s_qkv, s_out), (total[80:144], t_qkv, t_out)):
+        for m in range(3):
+            qkv_ref[m] = block[:, m * 128 : (m + 1) * 128]
+        out_ref[...] = block[:, 384:512]
+    sums_ref[...] = total[64:72]
+    d = place_ref[1]
+    pair = sums_ref[:, pl.ds(pl.multiple_of(d // 2 * 128, 128), 128)]
+    mine = jnp.where(d % 2 == 0, pair[:, 0:64], pair[:, 64:128])
+    for n, ref in enumerate(norms):
+        ref[...] = mine[n : n + 1]
+
+
+def finish(place, mine):
+    ins = [place, mine[0]] + [swap(mine[j], "tensor", j) for j in (1, 2, 3)]
+    outs = [shape((3, 64, 128), F32), shape((64, 128), F32)] * 2 + [shape((1, 64), F32)] * 6
+    return run(
+        finish_kernel, 0.01, (1,), ins, [SMEM] + whole_specs(ins[1:]), outs, whole_specs(outs), [pltpu.VMEM((8, 512), F32)]
+    )
 
 
 def scatter_grad(grads):
@@ -1056,25 +1063,23 @@
     zero = jnp.zeros_like(t_dg)
     s_even, s_odd = space_grad(
         place, a, dqkv, low, s_o, (s_dg, d_dg, s_db, d_db, t_dg, zero, t_db, zero, ff_dg, zero, ff_db, zero),
-        (dx0_disc, ff_mine, *t_parts) if direct else (),
+        (dx0_disc, *t_parts) if direct else (),
     )
 
     part = width // tensor
     if direct:
-        ff_share = reduce_tensor(ff_mine)
-        both = jnp.concatenate([gen_aspect, disc_aspect])
-        outs = join_raster(place, both, y, (y_gen, y_disc), (s_even, ff_share))
-        near = reduce_core(s_even, s_odd, (*gen_parts, *outs))
-        dx_gen = join_raster(place, gen_aspect, dx0_gen, (gen_parts,), near[:1])
-        ours = reduce_chips(chip_parts(near), t_parts, dx_gen)
-        dx_disc = join_raster(place, disc_aspect, dx0_disc, (disc_parts,), ours[:1])
-        share = reduce_tensor(ours)
-        small = share[64:70]
+        ff_share = lax.psum_scatter(ff_mine, "tensor", scatter_dimension=0).astype(F32)
+        y_gen = join_raster(place, gen_aspect, y, (y_gen,), 0, 6, (s_even,))
+        near = reduce_core(s_even, s_odd, (*gen_parts, *y_gen, disc_parts[0]))
+        dx_gen = join_raster(place, gen_aspect, dx0_gen, (gen_parts,), 0, JOIN, near[:1])
+        y_disc = join_raster(place, disc_aspect, y, (y_disc,), clips, JOIN, near[:1])
+        ours = reduce_chips(chip_parts(near), t_parts, (*dx_gen, *y_disc, ff_share))
+        dx_disc = join_raster(place, disc_aspect, dx0_disc, (disc_parts,), 0, JOIN, ours[:1])
+        s_qkv, s_out, t_qkv, t_out, *small = finish(place, ours)
+        shares = (s_qkv, s_out.T, t_qkv, t_out.T)
+        small = [n[0] for n in small]
         in_share, out_share = ff_share[:64], ff_share[64:]
-        shares = []
-        for block in (share[:64], share[80:]):
-            shares += [jnp.moveaxis(block[:, : 3 * part].reshape(-1, 3, part), 1, 0), block[:, 3 * part :].T]
-        y_gen, y_disc, dx_gen, dx_disc = (v.reshape(gen_tokens.shape) for v in (*outs, *dx_gen, *dx_disc))
+        y_gen, y_disc, dx_gen, dx_disc = (v.reshape(gen_tokens.shape) for v in (*y_gen, *y_disc, *dx_gen, *dx_disc))
     else:
         y_gen, y_disc, dx_gen, dx_disc = (
             gather_raster(v.reshape(clips, frames, AREA, width), aspect, split, patches)
@@ -1088,8 +1093,8 @@
             block = scatter_grad([in_order(even, odd).reshape(width, 4, tensor, part)])[0]
             shares += [jnp.moveaxis(block[:, :3], 1, 0), block[:, 3].T]
         small = lax.psum(s_even[0, 0, 64:70].astype(F32), ("dp", "tensor"))
-    piece = width // lax.axis_size("dp")
-    small = lax.dynamic_slice_in_dim(small, dp_at * piece, piece, 1)
+        piece = width // lax.axis_size("dp")
+        small = lax.dynamic_slice_in_dim(small, dp_at * piece, piece, 1)
 
     return (
         y_gen, dx_gen, y_disc, dx_disc,

time: 330 us -> 315 us (0.955)
  local copies, waits for them, and re-layouts: 19.5 us -> 11.5 us
  waiting for transfers between devices: 31.2 us -> 27 us
    ppermute x41 -> x38, waiting for transfers between devices: 31.1 us -> 26.8 us  [swap(): lax.ppermute(x, axis, [(i, i ^ way) for i in range(lax.axis_size(axis))])]
    ppermute x41 -> x38, starting transfers between devices: 66.4 us -> 63.2 us  [swap(): lax.ppermute(x, axis, [(i, i ^ way) for i in range(lax.axis_size(axis))])]
    unnamed x122 -> x102, local copies, waits for them, and re-layouts: 12.6 us -> 10.1 us
  transfers between devices with their start and end apart: 44 -> 42, of which waited for: 5 -> 5; matrix products, arithmetic and copies ran while one was open for 1% -> 1% of each run, Pallas kernels for 50% -> 53%
where the time goes in v1:
time: 315 us; the launch traced here: 311 us
  Pallas kernels  191 us (61%)
  starting transfers between devices  63.4 us (20%)
  waiting for transfers between devices  27 us (9%)
  between operations  16 us (5%)
  local copies, waits for them, and re-layouts  11.5 us (4%)
    pallas_call x24, Pallas kernels, run(): pl.pallas_call(body, grid=grid, in_specs=list(in_specs) + [ANY] * extra,...  191 us
    ppermute x38, starting transfers between devices, swap(): lax.ppermute(x, axis, [(i, i ^ way) for i in range(lax.axis_size(axis))])  63.2 us
    ppermute x38, waiting for transfers between devices, swap(): lax.ppermute(x, axis, [(i, i ^ way) for i in range(lax.axis_size(axis))])  26.8 us
    unnamed x102, local copies, waits for them, and re-layouts  10.1 us
  transfers between devices with their start and end apart: 42, of which 5 were waited for; matrix products, arithmetic and copies ran while one was open for 1% of the time, Pallas kernels for 53%

profile of v1, /device:TPU:0, one launch (start us, length us, event | category | flops | bytes accessed | tf_op | source)
XLA Modules:
  0.0 311.3 jit_solution(7705791752014537642)
XLA Ops:
  17.1 3.3 %shard_map.352 = (bf16[3,160,512]{2,1,0:T(8,128)(2,1)}, bf16[3,80,512]{2,1,0:T(8,128)(2,1)}, bf16[3,80,512]{2,1,0:T(8,128)(2,1)}) custom-call(s32[2]{0:T(128)} %pad_add_fusion.refs_0_.refs_2_, s32[3]{0:T(128)} %refs_1_.17, bf16[3,320,512]{2,1,0:T(8,128)(2,1)} %bitcast.45, bf16[128,512]{1,0:T(8,128)(2,1)} %get-tuple-element.112.refs_3_.refs_1_), custom_call_target="tpu_custom_call" | custom-call | flops 25000000 | tf_op jit(solution)/shard_map/pallas_call | solution.py:67
  20.4 3.3 %shard_map.353 = (bf16[3,160,512]{2,1,0:T(8,128)(2,1)}, bf16[3,80,512]{2,1,0:T(8,128)(2,1)}, bf16[3,80,512]{2,1,0:T(8,128)(2,1)}) custom-call(s32[2]{0:T(128)} %pad_add_fusion.refs_0_.refs_2_, s32[3]{0:T(128)} %refs_1_.19, bf16[3,320,512]{2,1,0:T(8,128)(2,1)} %bitcast.43, bf16[3,160,512]{2,1,0:T(8,128)(2,1)} %get-tuple-element.113.refs_3_, ...), custom_call_target="tpu_custom_call" | custom-call | flops 25000000 | tf_op jit(solution)/shard_map/pallas_call | solution.py:67
  23.7 4.0 %shard_map.354 = (bf16[3,320,512]{2,1,0:T(8,128)(2,1)}, bf16[3,160,512]{2,1,0:T(8,128)(2,1)}, bf16[3,80,512]{2,1,0:T(8,128)(2,1)}, bf16[3,80,512]{2,1,0:T(8,128)(2,1)}) custom-call(s32[2]{0:T(128)} %pad_add_fusion.refs_0_.refs_2_, s32[3]{0:T(128)} %refs_1_.17, s32[3]{0:T(128)} %refs_2_.3, f32[1]{0:T(128)S(6)} %div.3.refs_3_, bf16[3,320,512]{2,1,0:T(8,128)(2,1)} %bitcast.58, ...), custom_call_target="tpu_custom_call" | custom-call | flops 10000000000 | tf_op jit(solution)/shard_map/pallas_call | solution.py:67
  31.5 3.5 %collective-permute-start.10 = (bf16[128,512]{1,0:T(8,128)(2,1)S(1)}, bf16[128,512]{1,0:T(8,128)(2,1)S(1)}, u32[]{:S(2)}, u32[]{:S(2)}) collective-permute-start(bf16[128,512]{1,0:T(8,128)(2,1)S(1)} %copy-done.26), channel_id=1, source_target_pairs={{0,2},{1,3},{2,0},{3,1},{4,6},{5,7},{6,4},{7,5},{8,10},{9,11},{10,... | collective-permute-start | bytes 393224 | tf_op jit(solution)/shard_map/ppermute | solution.py:273
  38.9 7.1 %collective-permute-done.10.refs_3_ = bf16[128,512]{1,0:T(8,128)(2,1)S(1)} collective-permute-done((bf16[128,512]{1,0:T(8,128)(2,1)S(1)}, bf16[128,512]{1,0:T(8,128)(2,1)S(1)}, u32[]{:S(2)}, u32[]{:S(2)}) %collective-permute-start.10) | collective-permute-done | bytes 131104 | tf_op jit(solution)/shard_map/ppermute | solution.py:273
  46.0 4.0 %collective-permute-start.9 = (bf16[128,512]{1,0:T(8,128)(2,1)S(1)}, bf16[128,512]{1,0:T(8,128)(2,1)S(1)}, u32[]{:S(2)}, u32[]{:S(2)}) collective-permute-start(bf16[128,512]{1,0:T(8,128)(2,1)S(1)} %copy-done.26), channel_id=1, source_target_pairs={{0,1},{1,0},{2,3},{3,2},{4,5},{5,4},{6,7},{7,6},{8,9},{9,8},{10,11... | collective-permute-start | bytes 393224 | tf_op jit(solution)/shard_map/ppermute | solution.py:273
  50.5 11.9 %collective-permute-done.11.refs_4_ = bf16[128,512]{1,0:T(8,128)(2,1)S(1)} collective-permute-done((bf16[128,512]{1,0:T(8,128)(2,1)S(1)}, bf16[128,512]{1,0:T(8,128)(2,1)S(1)}, u32[]{:S(2)}, u32[]{:S(2)}) %collective-permute-start.11) | collective-permute-done | bytes 131104 | tf_op jit(solution)/shard_map/ppermute | solution.py:273
  62.5 5.6 %collective-permute-start = (bf16[3,160,512]{2,1,0:T(8,128)(2,1)S(1)}, bf16[3,160,512]{2,1,0:T(8,128)(2,1)S(1)}, u32[]{:S(2)}, u32[]{:S(2)}) collective-permute-start(bf16[3,160,512]{2,1,0:T(8,128)(2,1)S(1)} %copy-done.34), channel_id=1, source_target_pairs={{0,1},{1,0},{2,3},{3,2},{4,5},{5,4},{6,7},{7,6},{8,9},{9,8},{10,11... | collective-permute-start | bytes 1474568 | tf_op jit(solution)/shard_map/ppermute | solution.py:273
  75.1 9.3 %shard_map.357 = (f32[6,320,512]{2,1,0:T(8,128)}, bf16[6,320,1536]{2,1,0:T(8,128)(2,1)}, bf16[6,10,64,256]{3,2,1,0:T(8,128)(2,1)}, bf16[6,320,512]{2,1,0:T(8,128)(2,1)}, bf16[6,320,512]{2,1,0:T(8,128)(2,1)}) custom-call(s32[2]{0:T(128)} %pad_add_fusion.refs_0_.refs_2_, s32[3]{0:T(128)} %refs_1_.17, bf16[3,320,512]{2,1,0:T(8,128)(2,1)} %bitcast.46, ...), custom_call_target="tpu_custom_call" | custom-call | flops 24999999488 | tf_op jit(solution)/shard_map/pallas_call | solution.py:67
  84.4 10.2 %shard_map.358 = (f32[6,320,512]{2,1,0:T(8,128)}, bf16[6,320,1536]{2,1,0:T(8,128)(2,1)}, f32[6,320,128]{2,1,0:T(8,128)}, bf16[6,320,512]{2,1,0:T(8,128)(2,1)}) custom-call(f32[6,320,512]{2,1,0:T(8,128)} %get-tuple-element.121.refs_0_.refs_10_, f32[1,512]{1,0:T(1,128)} %bitcast.67, f32[1,512]{1,0:T(1,128)} %bitcast.70, bf16[8,4,128,512]{3,2,1,0:T(8,128)(2,1)} %bitcast.50), custom_call_target="tpu_custom_call" | custom-call | flops 24999999488 | tf_op jit(solution)/shard_map/pallas_call | solution.py:67
  97.6 8.9 %shard_map.359 = (f32[6,320,512]{2,1,0:T(8,128)}, bf16[6,320,1536]{2,1,0:T(8,128)(2,1)}, bf16[6,10,64,256]{3,2,1,0:T(8,128)(2,1)}, bf16[6,320,512]{2,1,0:T(8,128)(2,1)}, bf16[6,320,512]{2,1,0:T(8,128)(2,1)}) custom-call(s32[2]{0:T(128)} %pad_add_fusion.refs_0_.refs_2_, ...), custom_call_target="tpu_custom_call", output_to_operand_aliasing={{0}: (10, {}), {1}: (11, {}), {2}: (12, {}), {3}: (13, {}),... | custom-call | flops 24999999488 | tf_op jit(solution)/shard_map/pallas_call | solution.py:67
  106.6 10.5 %shard_map.360 = (f32[6,320,512]{2,1,0:T(8,128)}, bf16[6,320,1536]{2,1,0:T(8,128)(2,1)}, f32[6,320,128]{2,1,0:T(8,128)}, bf16[6,320,512]{2,1,0:T(8,128)(2,1)}) custom-call(f32[6,320,512]{2,1,0:T(8,128)} %get-tuple-element.127.refs_0_.refs_2_, f32[1,512]{1,0:T(1,128)} %bitcast.68, ...), custom_call_target="tpu_custom_call", output_to_operand_aliasing={{0}: (4, {}), {1}: (5, {}), {2}: (6, {}), {3}: (7, {})} | custom-call | flops 24999999488 | tf_op jit(solution)/shard_map/pallas_call | solution.py:67
  118.1 19.5 %shard_map.361 = (bf16[6,320,512]{2,1,0:T(8,128)(2,1)}, f32[6,320,512]{2,1,0:T(8,128)}, bf16[3,320,512]{2,1,0:T(8,128)(2,1)}, bf16[3,320,512]{2,1,0:T(8,128)(2,1...) custom-call(s32[2]{0:T(128)} %pad_add_fusion.refs_0_.refs_2_, ...), custom_call_target="tpu_custom_call" | custom-call | flops 49999998976 | tf_op jit(solution)/shard_map/pallas_call | solution.py:67
  142.1 31.8 %shard_map.362 = (bf16[6,320,512]{2,1,0:T(8,128)(2,1)}, f32[6,320,512]{2,1,0:T(8,128)}, bf16[8,4,128,512]{3,2,1,0:T(8,128)(2,1)}, f32[8,512]{1,0:T(8,128)}, f32[...) custom-call(f32[3]{0:T(128)} %add_convert_fusion.refs_0_, ...), custom_call_target="tpu_custom_call", output_to_operand_aliasing={{0}: (14, {}), {1}: (15, {})} | custom-call | flops 74999996416 | tf_op jit(solution)/shard_map/pallas_call | solution.py:67
  179.4 27.0 %shard_map.363 = (f32[6,320,512]{2,1,0:T(8,128)}, f32[8,512]{1,0:T(8,128)}, f32[8,512]{1,0:T(8,128)}, bf16[4,4,64,512]{3,2,1,0:T(8,128)(2,1)}, bf16[4,4,64,512]{3,2,1,0:T(8,128)(2,1)}) custom-call(s32[2]{0:T(128)} %pad_add_fusion.refs_0_.refs_2_, f32[6,320,512]{2,1,0:T(8,128)} %get-tuple-element.147.refs_1_, ...), custom_call_target="tpu_custom_call" | custom-call | flops 65000001536 | tf_op jit(solution)/shard_map/pallas_call | solution.py:67
  207.4 10.2 %shard_map.364 = (bf16[6,320,1536]{2,1,0:T(8,128)(2,1)}, bf16[6,320,512]{2,1,0:T(8,128)(2,1)}, bf16[6,320,512]{2,1,0:T(8,128)(2,1)}, bf16[3,320,512]{2,1,0:T(8,1...) custom-call(f32[6,320,512]{2,1,0:T(8,128)} %get-tuple-element.151.re, ...), custom_call_target="tpu_custom_call" | custom-call | flops 24999999488 | tf_op jit(solution)/shard_map/pallas_call | solution.py:67
  227.3 10.3 %shard_map.366 = (bf16[6,320,1536]{2,1,0:T(8,128)(2,1)}, bf16[6,320,512]{2,1,0:T(8,128)(2,1)}, bf16[6,320,512]{2,1,0:T(8,128)(2,1)}, bf16[3,320,512]{2,1,0:T(8,1...) custom-call(f32[6,320,512]{2,1,0:T(8,128)} %get-tuple-element.151.re, ...), custom_call_target="tpu_custom_call", output_to_operand_aliasing={{0}: (8, {}), {1}: (9, {}), {2}: (10, {})} | custom-call | flops 24999999488 | tf_op jit(solution)/shard_map/pallas_call | solution.py:67
  240.3 11.5 %shard_map.367 = (bf16[4,4,80,512]{3,2,1,0:T(8,128)(2,1)}, bf16[4,4,80,512]{3,2,1,0:T(8,128)(2,1)}) custom-call(s32[2]{0:T(128)} %pad_add_fusion.refs_0_.refs_2_, bf16[1920,512]{1,0:T(8,128)(2,1)} %bitcast.89, bf16[1920,1536]{1,0:T(8,128)(2,1)} %bitcast.87, bf16[1920,512]{1,0:T(8,128)(2,1)} %bitcast.88, bf16[1920,512]{1,0:T(8,128)(2,1)} %bitcast.90, ...), custom_call_target="tpu_custom_call" | custom-call | flops 15000000512 | tf_op jit(solution)/shard_map/pallas_call | solution.py:67
  251.8 3.7 %shard_map.368.refs_5_ = bf16[3,320,512]{2,1,0:T(8,128)(2,1)} custom-call(s32[2]{0:T(128)} %pad_add_fusion.refs_0_.refs_2_, s32[3]{0:T(128)} %refs_1_.17, bf16[6,320,512]{2,1,0:T(8,128)(2,1)} %get-tuple-element.143.refs_2_, bf16[3,160,512]{2,1,0:T(8,128)(2,1)} %copy-done.33, bf16[3,80,512]{2,1,0:T(8,128)(2,1)} %copy-done.37, bf16[3,80,512]{2,1,0:T(8,128)(2,1)} %copy-done.38, ...), custom_call_target="tpu_custom_call" | custom-call | flops 15000000512 | tf_op jit(solution)/shard_map/pallas_call | solution.py:67
  268.4 3.7 %shard_map.371.refs_9_ = bf16[3,320,512]{2,1,0:T(8,128)(2,1)} custom-call(s32[2]{0:T(128)} %pad_add_fusion.refs_0_.refs_2_, s32[3]{0:T(128)} %refs_1_.19, bf16[6,320,512]{2,1,0:T(8,128)(2,1)} %get-tuple-element.143.refs_2_, bf16[3,160,512]{2,1,0:T(8,128)(2,1)} %copy-done.6, bf16[3,80,512]{2,1,0:T(8,128)(2,1)} %copy-done.15, bf16[3,80,512]{2,1,0:T(8,128)(2,1)} %copy-done.16, ...), custom_call_target="tpu_custom_call" | custom-call | flops 25000000 | tf_op jit(solution)/shard_map/pallas_call | solution.py:67
  272.2 3.7 %shard_map.370.refs_8_ = bf16[3,320,512]{2,1,0:T(8,128)(2,1)} custom-call(s32[2]{0:T(128)} %pad_add_fusion.refs_0_.refs_2_, s32[3]{0:T(128)} %refs_1_.17, bf16[3,320,512]{2,1,0:T(8,128)(2,1)} %get-tuple-element.160.refs_2_, bf16[3,160,512]{2,1,0:T(8,128)(2,1)} %copy-done, bf16[3,80,512]{2,1,0:T(8,128)(2,1)} %copy-done.4, bf16[3,80,512]{2,1,0:T(8,128)(2,1)} %copy-done.5, ...), custom_call_target="tpu_custom_call" | custom-call | flops 25000000 | tf_op jit(solution)/shard_map/pallas_call | solution.py:67
  282.7 6.1 %collective-permute-start.35 = (bf16[144,512]{1,0:T(8,128)(2,1)}, bf16[144,512]{1,0:T(8,128)(2,1)S(1)}, u32[]{:S(2)}, u32[]{:S(2)}) collective-permute-start(bf16[144,512]{1,0:T(8,128)(2,1)} %get-tuple-element.195), channel_id=1, source_target_pairs={{0,1},{1,0},{2,3},{3,2},{4,5},{5,4},{6,7},{7,6},{8,9},{9,8},{10,11... | collective-permute-start | bytes 442376 | tf_op jit(solution)/shard_map/ppermute | solution.py:273
  292.2 3.7 %shard_map.373 = bf16[3,320,512]{2,1,0:T(8,128)(2,1)} custom-call(s32[2]{0:T(128)} %pad_add_fusion.refs_0_.refs_2_, s32[3]{0:T(128)} %refs_1_.19, bf16[3,320,512]{2,1,0:T(8,128)(2,1)} %get-tuple-element.177.refs_17_.refs_2_, bf16[3,160,512]{2,1,0:T(8,128)(2,1)} %copy-done.1, bf16[3,80,512]{2,1,0:T(8,128)(2,1)} %copy-done.19, bf16[3,80,512]{2,1,0:T(8,128)(2,1)} %copy-done.20, ...), custom_call_target="tpu_custom_call" | custom-call | flops 25000000 | tf_op jit(solution)/shard_map/pallas_call | solution.py:67
  296.6 4.7 %collective-permute-done.36.refs_3_ = bf16[144,512]{1,0:T(8,128)(2,1)S(1)} collective-permute-done((bf16[144,512]{1,0:T(8,128)(2,1)}, bf16[144,512]{1,0:T(8,128)(2,1)S(1)}, u32[]{:S(2)}, u32[]{:S(2)}) %collective-permute-start.36) | collective-permute-done | bytes 147488 | tf_op jit(solution)/shard_map/ppermute | solution.py:273
  (195 shorter events, 77.8 us)
Async XLA Ops:
  7.2 67.9 %all-gather.5.cloned.1.call-start = ((), (), s32[]{:S(2)}) async-start(), calls=%async_computation.4 | async-start | bytes 4718592 | tf_op jit(solution)/shard_map/all_gather | solution.py:1019
  30.4 86.7 %all-gather.7.cloned.1.call-start = ((), (), s32[]{:S(2)}) async-start(), calls=%async_computation.5 | async-start | bytes 4718592 | tf_op jit(solution)/shard_map/all_gather | solution.py:1023
  30.5 41.1 %collective-permute-start.6 = (bf16[3,160,512]{2,1,0:T(8,128)(2,1)S(1)}, bf16[3,160,512]{2,1,0:T(8,128)(2,1)S(1)}, u32[]{:S(2)}, u32[]{:S(2)}) collective-permute-start(bf16[3,160,512]{2,1,0:T(8,128)(2,1)S(1)} %copy-done.7), channel_id=1, source_target_pairs={{0,1},{1,0},{2,3},{3,2},{4,5},{5,4},{6,7},{7,6},{8,9},{9,8},{10,11... | collective-permute-start | bytes 1474568 | tf_op jit(solution)/shard_map/ppermute | solution.py:273
  35.0 33.6 %collective-permute-start.7 = (bf16[3,80,512]{2,1,0:T(8,128)(2,1)S(1)}, bf16[3,80,512]{2,1,0:T(8,128)(2,1)S(1)}, u32[]{:S(2)}, u32[]{:S(2)}) collective-permute-start(bf16[3,80,512]{2,1,0:T(8,128)(2,1)S(1)} %copy-done.18), channel_id=1, source_target_pairs={{0,2},{1,3},{2,0},{3,1},{4,6},{5,7},{6,4},{7,5},{8,10},{9,11},{10,... | collective-permute-start | bytes 737288 | tf_op jit(solution)/shard_map/ppermute | solution.py:273
  35.0 35.5 %collective-permute-start.8 = (bf16[3,80,512]{2,1,0:T(8,128)(2,1)S(1)}, bf16[3,80,512]{2,1,0:T(8,128)(2,1)S(1)}, u32[]{:S(2)}, u32[]{:S(2)}) collective-permute-start(bf16[3,80,512]{2,1,0:T(8,128)(2,1)S(1)} %copy-done.17), channel_id=1, source_target_pairs={{0,3},{1,2},{2,1},{3,0},{4,7},{5,6},{6,5},{7,4},{8,11},{9,10},{10,... | collective-permute-start | bytes 737288 | tf_op jit(solution)/shard_map/ppermute | solution.py:273
  37.4 25.0 %collective-permute-start.11 = (bf16[128,512]{1,0:T(8,128)(2,1)S(1)}, bf16[128,512]{1,0:T(8,128)(2,1)S(1)}, u32[]{:S(2)}, u32[]{:S(2)}) collective-permute-start(bf16[128,512]{1,0:T(8,128)(2,1)S(1)} %copy-done.26), channel_id=1, source_target_pairs={{0,3},{1,2},{2,1},{3,0},{4,7},{5,6},{6,5},{7,4},{8,11},{9,10},{10,... | collective-permute-start | bytes 393224 | tf_op jit(solution)/shard_map/ppermute | solution.py:273
  62.5 34.3 %collective-permute-start = (bf16[3,160,512]{2,1,0:T(8,128)(2,1)S(1)}, bf16[3,160,512]{2,1,0:T(8,128)(2,1)S(1)}, u32[]{:S(2)}, u32[]{:S(2)}) collective-permute-start(bf16[3,160,512]{2,1,0:T(8,128)(2,1)S(1)} %copy-done.34), channel_id=1, source_target_pairs={{0,1},{1,0},{2,3},{3,2},{4,5},{5,4},{6,7},{7,6},{8,9},{9,8},{10,11... | collective-permute-start | bytes 1474568 | tf_op jit(solution)/shard_map/ppermute | solution.py:273
  68.0 26.7 %collective-permute-start.1 = (bf16[3,80,512]{2,1,0:T(8,128)(2,1)S(1)}, bf16[3,80,512]{2,1,0:T(8,128)(2,1)S(1)}, u32[]{:S(2)}, u32[]{:S(2)}) collective-permute-start(bf16[3,80,512]{2,1,0:T(8,128)(2,1)S(1)} %copy-done.43), channel_id=1, source_target_pairs={{0,2},{1,3},{2,0},{3,1},{4,6},{5,7},{6,4},{7,5},{8,10},{9,11},{10,... | collective-permute-start | bytes 737288 | tf_op jit(solution)/shard_map/ppermute | solution.py:273
  68.6 28.2 %collective-permute-start.2 = (bf16[3,80,512]{2,1,0:T(8,128)(2,1)S(1)}, bf16[3,80,512]{2,1,0:T(8,128)(2,1)S(1)}, u32[]{:S(2)}, u32[]{:S(2)}) collective-permute-start(bf16[3,80,512]{2,1,0:T(8,128)(2,1)S(1)} %copy-done.42), channel_id=1, source_target_pairs={{0,3},{1,2},{2,1},{3,0},{4,7},{5,6},{6,5},{7,4},{8,11},{9,10},{10,... | collective-permute-start | bytes 737288 | tf_op jit(solution)/shard_map/ppermute | solution.py:273
  70.5 46.6 %collective-permute-start.12 = (bf16[3,160,512]{2,1,0:T(8,128)(2,1)}, bf16[3,160,512]{2,1,0:T(8,128)(2,1)S(1)}, u32[]{:S(2)}, u32[]{:S(2)}) collective-permute-start(bf16[3,160,512]{2,1,0:T(8,128)(2,1)} %get-tuple-element.132), channel_id=1, source_target_pairs={{0,1},{1,0},{2,3},{3,2},{4,5},{5,4},{6,7},{7,6},{8,9},{9,8},{10,11... | collective-permute-start | bytes 1474568 | tf_op jit(solution)/shard_map/ppermute | solution.py:273
  71.6 45.4 %collective-permute-start.13 = (bf16[3,80,512]{2,1,0:T(8,128)(2,1)}, bf16[3,80,512]{2,1,0:T(8,128)(2,1)S(1)}, u32[]{:S(2)}, u32[]{:S(2)}) collective-permute-start(bf16[3,80,512]{2,1,0:T(8,128)(2,1)} %get-tuple-element.133), channel_id=1, source_target_pairs={{0,2},{1,3},{2,0},{3,1},{4,6},{5,7},{6,4},{7,5},{8,10},{9,11},{10,... | collective-permute-start | bytes 737288 | tf_op jit(solution)/shard_map/ppermute | solution.py:273
  75.0 176.8 %reduce-scatter.3.cloned.1.call-start = ((), (), s32[]{:S(2)}) async-start(), calls=%async_computation.2 | async-start | bytes 4718592 | tf_op jit(solution)/shard_map/reduce_scatter | solution.py:1049
  94.7 22.4 %collective-permute-start.14 = (bf16[3,80,512]{2,1,0:T(8,128)(2,1)S(1)}, bf16[3,80,512]{2,1,0:T(8,128)(2,1)S(1)}, u32[]{:S(2)}, u32[]{:S(2)}) collective-permute-start(bf16[3,80,512]{2,1,0:T(8,128)(2,1)S(1)} %copy-done.41), channel_id=1, source_target_pairs={{0,3},{1,2},{2,1},{3,0},{4,7},{5,6},{6,5},{7,4},{8,11},{9,10},{10,... | collective-permute-start | bytes 737288 | tf_op jit(solution)/shard_map/ppermute | solution.py:273
  137.6 40.9 %collective-permute-start.15 = (bf16[3,160,512]{2,1,0:T(8,128)(2,1)}, bf16[3,160,512]{2,1,0:T(8,128)(2,1)S(1)}, u32[]{:S(2)}, u32[]{:S(2)}) collective-permute-start(bf16[3,160,512]{2,1,0:T(8,128)(2,1)} %get-tuple-element.144), channel_id=1, source_target_pairs={{0,1},{1,0},{2,3},{3,2},{4,5},{5,4},{6,7},{7,6},{8,9},{9,8},{10,11... | collective-permute-start | bytes 1474568 | tf_op jit(solution)/shard_map/ppermute | solution.py:273
  138.2 38.8 %collective-permute-start.16 = (bf16[3,80,512]{2,1,0:T(8,128)(2,1)}, bf16[3,80,512]{2,1,0:T(8,128)(2,1)S(1)}, u32[]{:S(2)}, u32[]{:S(2)}) collective-permute-start(bf16[3,80,512]{2,1,0:T(8,128)(2,1)} %get-tuple-element.145), channel_id=1, source_target_pairs={{0,2},{1,3},{2,0},{3,1},{4,6},{5,7},{6,4},{7,5},{8,10},{9,11},{10,... | collective-permute-start | bytes 737288 | tf_op jit(solution)/shard_map/ppermute | solution.py:273
  140.6 37.9 %collective-permute-start.17 = (bf16[3,80,512]{2,1,0:T(8,128)(2,1)}, bf16[3,80,512]{2,1,0:T(8,128)(2,1)S(1)}, u32[]{:S(2)}, u32[]{:S(2)}) collective-permute-start(bf16[3,80,512]{2,1,0:T(8,128)(2,1)} %get-tuple-element.146), channel_id=1, source_target_pairs={{0,3},{1,2},{2,1},{3,0},{4,7},{5,6},{6,5},{7,4},{8,11},{9,10},{10,... | collective-permute-start | bytes 737288 | tf_op jit(solution)/shard_map/ppermute | solution.py:273
  173.9 32.6 %collective-permute-start.19 = (bf16[3,160,512]{2,1,0:T(8,128)(2,1)}, bf16[3,160,512]{2,1,0:T(8,128)(2,1)S(1)}, u32[]{:S(2)}, u32[]{:S(2)}) collective-permute-start(bf16[3,160,512]{2,1,0:T(8,128)(2,1)} %get-tuple-element.157), channel_id=1, source_target_pairs={{0,1},{1,0},{2,3},{3,2},{4,5},{5,4},{6,7},{7,6},{8,9},{9,8},{10,11... | collective-permute-start | bytes 1474568 | tf_op jit(solution)/shard_map/ppermute | solution.py:273
  174.0 32.5 %collective-permute-start.20 = (bf16[3,80,512]{2,1,0:T(8,128)(2,1)}, bf16[3,80,512]{2,1,0:T(8,128)(2,1)S(1)}, u32[]{:S(2)}, u32[]{:S(2)}) collective-permute-start(bf16[3,80,512]{2,1,0:T(8,128)(2,1)} %get-tuple-element.158), channel_id=1, source_target_pairs={{0,2},{1,3},{2,0},{3,1},{4,6},{5,7},{6,4},{7,5},{8,10},{9,11},{10,... | collective-permute-start | bytes 737288 | tf_op jit(solution)/shard_map/ppermute | solution.py:273
  176.9 99.0 %reduce-scatter.5.cloned.1.call-start = ((), (), s32[]{:S(2)}) async-start(), calls=%async_computation.3 | async-start | bytes 655360 | tf_op jit(solution)/shard_map/reduce_scatter | solution.py:1071
  177.0 29.4 %collective-permute-start.21 = (bf16[3,80,512]{2,1,0:T(8,128)(2,1)S(1)}, bf16[3,80,512]{2,1,0:T(8,128)(2,1)S(1)}, u32[]{:S(2)}, u32[]{:S(2)}) collective-permute-start(bf16[3,80,512]{2,1,0:T(8,128)(2,1)S(1)} %copy-done.48), channel_id=1, source_target_pairs={{0,3},{1,2},{2,1},{3,0},{4,7},{5,6},{6,5},{7,4},{8,11},{9,10},{10,... | collective-permute-start | bytes 737288 | tf_op jit(solution)/shard_map/ppermute | solution.py:273
  217.6 38.1 %collective-permute-start.25 = (bf16[3,160,512]{2,1,0:T(8,128)(2,1)}, bf16[3,160,512]{2,1,0:T(8,128)(2,1)S(1)}, u32[]{:S(2)}, u32[]{:S(2)}) collective-permute-start(bf16[3,160,512]{2,1,0:T(8,128)(2,1)} %get-tuple-element.182), channel_id=1, source_target_pairs={{0,1},{1,0},{2,3},{3,2},{4,5},{5,4},{6,7},{7,6},{8,9},{9,8},{10,11... | collective-permute-start | bytes 1474568 | tf_op jit(solution)/shard_map/ppermute | solution.py:273
  217.7 37.9 %collective-permute-start.26 = (bf16[3,80,512]{2,1,0:T(8,128)(2,1)}, bf16[3,80,512]{2,1,0:T(8,128)(2,1)S(1)}, u32[]{:S(2)}, u32[]{:S(2)}) collective-permute-start(bf16[3,80,512]{2,1,0:T(8,128)(2,1)} %get-tuple-element.183), channel_id=1, source_target_pairs={{0,2},{1,3},{2,0},{3,1},{4,6},{5,7},{6,4},{7,5},{8,10},{9,11},{10,... | collective-permute-start | bytes 737288 | tf_op jit(solution)/shard_map/ppermute | solution.py:273
  265.1 26.3 %collective-permute-start.30 = (bf16[3,80,512]{2,1,0:T(8,128)(2,1)S(1)}, bf16[3,80,512]{2,1,0:T(8,128)(2,1)S(1)}, u32[]{:S(2)}, u32[]{:S(2)}) collective-permute-start(bf16[3,80,512]{2,1,0:T(8,128)(2,1)S(1)} %copy-done.40), channel_id=1, source_target_pairs={{0,2},{1,3},{2,0},{3,1},{4,6},{5,7},{6,4},{7,5},{8,10},{9,11},{10,... | collective-permute-start | bytes 737288 | tf_op jit(solution)/shard_map/ppermute | solution.py:273
  266.7 24.7 %collective-permute-start.31 = (bf16[3,80,512]{2,1,0:T(8,128)(2,1)S(1)}, bf16[3,80,512]{2,1,0:T(8,128)(2,1)S(1)}, u32[]{:S(2)}, u32[]{:S(2)}) collective-permute-start(bf16[3,80,512]{2,1,0:T(8,128)(2,1)S(1)} %copy-done.39), channel_id=1, source_target_pairs={{0,3},{1,2},{2,1},{3,0},{4,7},{5,6},{6,5},{7,4},{8,11},{9,10},{10,... | collective-permute-start | bytes 737288 | tf_op jit(solution)/shard_map/ppermute | solution.py:273
  (69 other events, 582.9 us)
Sparse Core Ops, SparseCore 0:
  30.6 38.1 all-gather.4
  75.1 36.2 all-gather.6
  177.0 50.4 reduce-scatter.2
  252.0 23.6 reduce-scatter.4

commit v2 on v1

--- a/solution.py
+++ b/solution.py
@@ -53,7 +53,7 @@
     return jnp.sum(values.reshape(-1, 8, values.shape[-1]), axis=0)
 
 
-ANY = pl.BlockSpec(memory_space=pl.ANY)
+HBM = pl.BlockSpec(memory_space=pltpu.HBM)
 SMEM = pl.BlockSpec(memory_space=pltpu.SMEM)
 
 
@@ -67,7 +67,7 @@
     return pl.pallas_call(
         body,
         grid=grid,
-        in_specs=list(in_specs) + [ANY] * extra,
+        in_specs=list(in_specs) + [HBM] * extra,
         out_specs=list(out_specs),
         out_shape=list(outs),
         scratch_shapes=list(scratch),
@@ -484,18 +484,20 @@
     return jnp.where(rows == cols, 1.0, 0.0).astype(BF16)
 
 
-def head_sums(products, selector):
+def head_sums(products, selector, exact):
     high = products.astype(BF16)
+    if not exact:
+        return dot(high, selector)
     rest = (products - high.astype(F32)).astype(BF16)
     return dot(high, selector) + dot(rest, selector)
 
 
-def time_scores(frames, left, right):
+def time_scores(frames, left, right, exact=True):
     totals = [None] * frames
     for t in range(frames):
         lhs = left(t).astype(F32)
         stacked = jnp.concatenate([lhs * right(f).astype(F32) for f in range(t + 1)], axis=0)
-        sums = head_sums(stacked, head_select(t))
+        sums = head_sums(stacked, head_select(t), exact)
         for f in range(t + 1):
             part = sums[f * AREA : (f + 1) * AREA]
             totals[f] = part if totals[f] is None else totals[f] + part
@@ -565,7 +567,7 @@
     def grads(t):
         return do_ref[t * AREA : (t + 1) * AREA, :]
 
-    dp = time_scores(frames, grads, values)
+    dp = time_scores(frames, grads, values, False)
     probs = [p_ref[0, f * AREA : (f + 1) * AREA, :] for f in range(frames)]
     inner = sum(p * d for p, d in zip(probs, dp))
     ds = [(p * (d - inner)).astype(BF16) for p, d in zip(probs, dp)]
@@ -1070,7 +1072,7 @@
     if direct:
         ff_share = lax.psum_scatter(ff_mine, "tensor", scatter_dimension=0).astype(F32)
         y_gen = join_raster(place, gen_aspect, y, (y_gen,), 0, 6, (s_even,))
-        near = reduce_core(s_even, s_odd, (*gen_parts, *y_gen, disc_parts[0]))
+        near = reduce_core(s_even, s_odd, (*gen_parts, *y_gen, *disc_parts[:2]))
         dx_gen = join_raster(place, gen_aspect, dx0_gen, (gen_parts,), 0, JOIN, near[:1])
         y_disc = join_raster(place, disc_aspect, y, (y_disc,), clips, JOIN, near[:1])
         ours = reduce_chips(chip_parts(near), t_parts, (*dx_gen, *y_disc, ff_share))

time: 315 us -> 312 us (level)
  waiting for transfers between devices: 27 us -> 31.2 us
  starting transfers between devices: 63.4 us -> 59.3 us
    ppermute x38, waiting for transfers between devices: 26.8 us -> 31.1 us  [swap(): lax.ppermute(x, axis, [(i, i ^ way) for i in range(lax.axis_size(axis))])]
    ppermute x38, starting transfers between devices: 63.2 us -> 59.2 us  [swap(): lax.ppermute(x, axis, [(i, i ^ way) for i in range(lax.axis_size(axis))])]
    unnamed x102 -> x100, local copies, waits for them, and re-layouts: 10.1 us -> 10 us
  transfers between devices with their start and end apart: 42 -> 42, of which waited for: 5 -> 7; matrix products, arithmetic and copies ran while one was open for 1% -> 1% of each run, Pallas kernels for 53% -> 53%
where the time goes in v2:
time: 312 us; the launch traced here: 308 us
  Pallas kernels  188 us (60%)
  starting transfers between devices  59.3 us (19%)
  waiting for transfers between devices  31.2 us (10%)
  between operations  16 us (5%)
  local copies, waits for them, and re-layouts  11.4 us (4%)
    pallas_call x24, Pallas kernels, run(): pl.pallas_call(body, grid=grid, in_specs=list(in_specs) + [HBM] * extra,...  188 us
    ppermute x38, starting transfers between devices, swap(): lax.ppermute(x, axis, [(i, i ^ way) for i in range(lax.axis_size(axis))])  59.2 us
    ppermute x38, waiting for transfers between devices, swap(): lax.ppermute(x, axis, [(i, i ^ way) for i in range(lax.axis_size(axis))])  31.1 us
    unnamed x100, local copies, waits for them, and re-layouts  10 us
  transfers between devices with their start and end apart: 42, of which 7 were waited for; matrix products, arithmetic and copies ran while one was open for 1% of the time, Pallas kernels for 53%

profile of v2, /device:TPU:0, one launch (start us, length us, event | category | flops | bytes accessed | tf_op | source)
XLA Modules:
  0.0 308.4 jit_solution(9728555373262508447)
XLA Ops:
  10.1 3.0 collective-permute-start.3
  17.0 3.3 %shard_map.352 = (bf16[3,160,512]{2,1,0:T(8,128)(2,1)}, bf16[3,80,512]{2,1,0:T(8,128)(2,1)}, bf16[3,80,512]{2,1,0:T(8,128)(2,1)}) custom-call(s32[2]{0:T(128)} %pad_add_fusion.refs_0_.refs_2_, s32[3]{0:T(128)} %refs_1_.17, bf16[3,320,512]{2,1,0:T(8,128)(2,1)} %bitcast.44, bf16[128,512]{1,0:T(8,128)(2,1)} %get-tuple-element.112.refs_3_.refs_1_), custom_call_target="tpu_custom_call" | custom-call | flops 25000000 | tf_op jit(solution)/shard_map/pallas_call | solution.py:67
  20.4 3.3 %shard_map.353 = (bf16[3,160,512]{2,1,0:T(8,128)(2,1)}, bf16[3,80,512]{2,1,0:T(8,128)(2,1)}, bf16[3,80,512]{2,1,0:T(8,128)(2,1)}) custom-call(s32[2]{0:T(128)} %pad_add_fusion.refs_0_.refs_2_, s32[3]{0:T(128)} %refs_1_.19, bf16[3,320,512]{2,1,0:T(8,128)(2,1)} %bitcast.42, bf16[3,160,512]{2,1,0:T(8,128)(2,1)} %get-tuple-element.113.refs_3_, ...), custom_call_target="tpu_custom_call" | custom-call | flops 25000000 | tf_op jit(solution)/shard_map/pallas_call | solution.py:67
  23.7 4.0 %shard_map.354 = (bf16[3,320,512]{2,1,0:T(8,128)(2,1)}, bf16[3,160,512]{2,1,0:T(8,128)(2,1)}, bf16[3,80,512]{2,1,0:T(8,128)(2,1)}, bf16[3,80,512]{2,1,0:T(8,128)(2,1)}) custom-call(s32[2]{0:T(128)} %pad_add_fusion.refs_0_.refs_2_, s32[3]{0:T(128)} %refs_1_.17, s32[3]{0:T(128)} %refs_2_.3, f32[1]{0:T(128)S(6)} %div.3.refs_3_, bf16[3,320,512]{2,1,0:T(8,128)(2,1)} %bitcast.58, ...), custom_call_target="tpu_custom_call" | custom-call | flops 10000000000 | tf_op jit(solution)/shard_map/pallas_call | solution.py:67
  31.4 3.5 %collective-permute-start.10 = (bf16[128,512]{1,0:T(8,128)(2,1)S(1)}, bf16[128,512]{1,0:T(8,128)(2,1)S(1)}, u32[]{:S(2)}, u32[]{:S(2)}) collective-permute-start(bf16[128,512]{1,0:T(8,128)(2,1)S(1)} %copy-done.26), channel_id=1, source_target_pairs={{0,2},{1,3},{2,0},{3,1},{4,6},{5,7},{6,4},{7,5},{8,10},{9,11},{10,... | collective-permute-start | bytes 393224 | tf_op jit(solution)/shard_map/ppermute | solution.py:273
  38.8 7.1 %collective-permute-done.10.refs_3_ = bf16[128,512]{1,0:T(8,128)(2,1)S(1)} collective-permute-done((bf16[128,512]{1,0:T(8,128)(2,1)S(1)}, bf16[128,512]{1,0:T(8,128)(2,1)S(1)}, u32[]{:S(2)}, u32[]{:S(2)}) %collective-permute-start.10) | collective-permute-done | bytes 131104 | tf_op jit(solution)/shard_map/ppermute | solution.py:273
  46.0 4.0 %collective-permute-start.9 = (bf16[128,512]{1,0:T(8,128)(2,1)S(1)}, bf16[128,512]{1,0:T(8,128)(2,1)S(1)}, u32[]{:S(2)}, u32[]{:S(2)}) collective-permute-start(bf16[128,512]{1,0:T(8,128)(2,1)S(1)} %copy-done.26), channel_id=1, source_target_pairs={{0,1},{1,0},{2,3},{3,2},{4,5},{5,4},{6,7},{7,6},{8,9},{9,8},{10,11... | collective-permute-start | bytes 393224 | tf_op jit(solution)/shard_map/ppermute | solution.py:273
  50.5 11.9 %collective-permute-done.11.refs_4_ = bf16[128,512]{1,0:T(8,128)(2,1)S(1)} collective-permute-done((bf16[128,512]{1,0:T(8,128)(2,1)S(1)}, bf16[128,512]{1,0:T(8,128)(2,1)S(1)}, u32[]{:S(2)}, u32[]{:S(2)}) %collective-permute-start.11) | collective-permute-done | bytes 131104 | tf_op jit(solution)/shard_map/ppermute | solution.py:273
  62.5 5.5 %collective-permute-start = (bf16[3,160,512]{2,1,0:T(8,128)(2,1)S(1)}, bf16[3,160,512]{2,1,0:T(8,128)(2,1)S(1)}, u32[]{:S(2)}, u32[]{:S(2)}) collective-permute-start(bf16[3,160,512]{2,1,0:T(8,128)(2,1)S(1)} %copy-done.34), channel_id=1, source_target_pairs={{0,1},{1,0},{2,3},{3,2},{4,5},{5,4},{6,7},{7,6},{8,9},{9,8},{10,11... | collective-permute-start | bytes 1474568 | tf_op jit(solution)/shard_map/ppermute | solution.py:273
  75.1 9.3 %shard_map.357 = (f32[6,320,512]{2,1,0:T(8,128)}, bf16[6,320,1536]{2,1,0:T(8,128)(2,1)}, bf16[6,10,64,256]{3,2,1,0:T(8,128)(2,1)}, bf16[6,320,512]{2,1,0:T(8,128)(2,1)}, bf16[6,320,512]{2,1,0:T(8,128)(2,1)}) custom-call(s32[2]{0:T(128)} %pad_add_fusion.refs_0_.refs_2_, s32[3]{0:T(128)} %refs_1_.17, bf16[3,320,512]{2,1,0:T(8,128)(2,1)} %bitcast.45, ...), custom_call_target="tpu_custom_call" | custom-call | flops 24999999488 | tf_op jit(solution)/shard_map/pallas_call | solution.py:67
  84.4 10.2 %shard_map.358 = (f32[6,320,512]{2,1,0:T(8,128)}, bf16[6,320,1536]{2,1,0:T(8,128)(2,1)}, f32[6,320,128]{2,1,0:T(8,128)}, bf16[6,320,512]{2,1,0:T(8,128)(2,1)}) custom-call(f32[6,320,512]{2,1,0:T(8,128)} %get-tuple-element.121.refs_0_.refs_10_, f32[1,512]{1,0:T(1,128)} %bitcast.67, f32[1,512]{1,0:T(1,128)} %bitcast.70, bf16[8,4,128,512]{3,2,1,0:T(8,128)(2,1)} %bitcast.50), custom_call_target="tpu_custom_call" | custom-call | flops 24999999488 | tf_op jit(solution)/shard_map/pallas_call | solution.py:67
  97.6 8.9 %shard_map.359 = (f32[6,320,512]{2,1,0:T(8,128)}, bf16[6,320,1536]{2,1,0:T(8,128)(2,1)}, bf16[6,10,64,256]{3,2,1,0:T(8,128)(2,1)}, bf16[6,320,512]{2,1,0:T(8,128)(2,1)}, bf16[6,320,512]{2,1,0:T(8,128)(2,1)}) custom-call(s32[2]{0:T(128)} %pad_add_fusion.refs_0_.refs_2_, ...), custom_call_target="tpu_custom_call", output_to_operand_aliasing={{0}: (10, {}), {1}: (11, {}), {2}: (12, {}), {3}: (13, {}),... | custom-call | flops 24999999488 | tf_op jit(solution)/shard_map/pallas_call | solution.py:67
  106.5 10.5 %shard_map.360 = (f32[6,320,512]{2,1,0:T(8,128)}, bf16[6,320,1536]{2,1,0:T(8,128)(2,1)}, f32[6,320,128]{2,1,0:T(8,128)}, bf16[6,320,512]{2,1,0:T(8,128)(2,1)}) custom-call(f32[6,320,512]{2,1,0:T(8,128)} %get-tuple-element.127.refs_0_.refs_2_, f32[1,512]{1,0:T(1,128)} %bitcast.68, ...), custom_call_target="tpu_custom_call", output_to_operand_aliasing={{0}: (4, {}), {1}: (5, {}), {2}: (6, {}), {3}: (7, {})} | custom-call | flops 24999999488 | tf_op jit(solution)/shard_map/pallas_call | solution.py:67
  118.0 19.5 %shard_map.361 = (bf16[6,320,512]{2,1,0:T(8,128)(2,1)}, f32[6,320,512]{2,1,0:T(8,128)}, bf16[3,320,512]{2,1,0:T(8,128)(2,1)}, bf16[3,320,512]{2,1,0:T(8,128)(2,1...) custom-call(s32[2]{0:T(128)} %pad_add_fusion.refs_0_.refs_2_, ...), custom_call_target="tpu_custom_call" | custom-call | flops 49999998976 | tf_op jit(solution)/shard_map/pallas_call | solution.py:67
  142.0 31.8 %shard_map.362 = (bf16[6,320,512]{2,1,0:T(8,128)(2,1)}, f32[6,320,512]{2,1,0:T(8,128)}, bf16[8,4,128,512]{3,2,1,0:T(8,128)(2,1)}, f32[8,512]{1,0:T(8,128)}, f32[...) custom-call(f32[3]{0:T(128)} %add_convert_fusion.refs_0_, ...), custom_call_target="tpu_custom_call", output_to_operand_aliasing={{0}: (14, {}), {1}: (15, {})} | custom-call | flops 74999996416 | tf_op jit(solution)/shard_map/pallas_call | solution.py:67
  179.3 24.0 %shard_map.363 = (f32[6,320,512]{2,1,0:T(8,128)}, f32[8,512]{1,0:T(8,128)}, f32[8,512]{1,0:T(8,128)}, bf16[4,4,64,512]{3,2,1,0:T(8,128)(2,1)}, bf16[4,4,64,512]{3,2,1,0:T(8,128)(2,1)}) custom-call(s32[2]{0:T(128)} %pad_add_fusion.refs_0_.refs_2_, f32[6,320,512]{2,1,0:T(8,128)} %get-tuple-element.147.refs_1_, ...), custom_call_target="tpu_custom_call" | custom-call | flops 65000001536 | tf_op jit(solution)/shard_map/pallas_call | solution.py:67
  204.4 10.2 %shard_map.364 = (bf16[6,320,1536]{2,1,0:T(8,128)(2,1)}, bf16[6,320,512]{2,1,0:T(8,128)(2,1)}, bf16[6,320,512]{2,1,0:T(8,128)(2,1)}, bf16[3,320,512]{2,1,0:T(8,1...) custom-call(f32[6,320,512]{2,1,0:T(8,128)} %get-tuple-element.151.re, ...), custom_call_target="tpu_custom_call" | custom-call | flops 24999999488 | tf_op jit(solution)/shard_map/pallas_call | solution.py:67
  224.4 10.3 %shard_map.366 = (bf16[6,320,1536]{2,1,0:T(8,128)(2,1)}, bf16[6,320,512]{2,1,0:T(8,128)(2,1)}, bf16[6,320,512]{2,1,0:T(8,128)(2,1)}, bf16[3,320,512]{2,1,0:T(8,1...) custom-call(f32[6,320,512]{2,1,0:T(8,128)} %get-tuple-element.151.re, ...), custom_call_target="tpu_custom_call", output_to_operand_aliasing={{0}: (8, {}), {1}: (9, {}), {2}: (10, {})} | custom-call | flops 24999999488 | tf_op jit(solution)/shard_map/pallas_call | solution.py:67
  241.4 11.5 %shard_map.367 = (bf16[4,4,80,512]{3,2,1,0:T(8,128)(2,1)}, bf16[4,4,80,512]{3,2,1,0:T(8,128)(2,1)}) custom-call(s32[2]{0:T(128)} %pad_add_fusion.refs_0_.refs_2_, bf16[1920,512]{1,0:T(8,128)(2,1)} %bitcast.89, bf16[1920,1536]{1,0:T(8,128)(2,1)} %bitcast.87, bf16[1920,512]{1,0:T(8,128)(2,1)} %bitcast.88, bf16[1920,512]{1,0:T(8,128)(2,1)} %bitcast.90, ...), custom_call_target="tpu_custom_call" | custom-call | flops 15000000512 | tf_op jit(solution)/shard_map/pallas_call | solution.py:67
  253.0 3.7 %shard_map.368.refs_5_ = bf16[3,320,512]{2,1,0:T(8,128)(2,1)} custom-call(s32[2]{0:T(128)} %pad_add_fusion.refs_0_.refs_2_, s32[3]{0:T(128)} %refs_1_.17, bf16[6,320,512]{2,1,0:T(8,128)(2,1)} %get-tuple-element.143.refs_2_, bf16[3,160,512]{2,1,0:T(8,128)(2,1)} %copy-done.33, bf16[3,80,512]{2,1,0:T(8,128)(2,1)} %copy-done.37, bf16[3,80,512]{2,1,0:T(8,128)(2,1)} %copy-done.38, ...), custom_call_target="tpu_custom_call" | custom-call | flops 15000000512 | tf_op jit(solution)/shard_map/pallas_call | solution.py:67
  269.4 3.7 %shard_map.371.refs_9_ = bf16[3,320,512]{2,1,0:T(8,128)(2,1)} custom-call(s32[2]{0:T(128)} %pad_add_fusion.refs_0_.refs_2_, s32[3]{0:T(128)} %refs_1_.19, bf16[6,320,512]{2,1,0:T(8,128)(2,1)} %get-tuple-element.143.refs_2_, bf16[3,160,512]{2,1,0:T(8,128)(2,1)} %copy-done.7, bf16[3,80,512]{2,1,0:T(8,128)(2,1)} %copy-done.16, bf16[3,80,512]{2,1,0:T(8,128)(2,1)} %copy-done.17, ...), custom_call_target="tpu_custom_call" | custom-call | flops 25000000 | tf_op jit(solution)/shard_map/pallas_call | solution.py:67
  273.1 3.7 %shard_map.370.refs_8_ = bf16[3,320,512]{2,1,0:T(8,128)(2,1)} custom-call(s32[2]{0:T(128)} %pad_add_fusion.refs_0_.refs_2_, s32[3]{0:T(128)} %refs_1_.17, bf16[3,320,512]{2,1,0:T(8,128)(2,1)} %get-tuple-element.160.refs_2_, bf16[3,160,512]{2,1,0:T(8,128)(2,1)} %copy-done, bf16[3,80,512]{2,1,0:T(8,128)(2,1)} %copy-done.4, bf16[3,80,512]{2,1,0:T(8,128)(2,1)} %copy-done.6, ...), custom_call_target="tpu_custom_call" | custom-call | flops 25000000 | tf_op jit(solution)/shard_map/pallas_call | solution.py:67
  289.7 3.7 %shard_map.373 = bf16[3,320,512]{2,1,0:T(8,128)(2,1)} custom-call(s32[2]{0:T(128)} %pad_add_fusion.refs_0_.refs_2_, s32[3]{0:T(128)} %refs_1_.19, bf16[3,320,512]{2,1,0:T(8,128)(2,1)} %get-tuple-element.177.refs_17_.refs_2_, bf16[3,160,512]{2,1,0:T(8,128)(2,1)} %copy-done.1, bf16[3,80,512]{2,1,0:T(8,128)(2,1)} %copy-done.5, bf16[3,80,512]{2,1,0:T(8,128)(2,1)} %copy-done.20, ...), custom_call_target="tpu_custom_call" | custom-call | flops 25000000 | tf_op jit(solution)/shard_map/pallas_call | solution.py:67
  294.1 4.3 %collective-permute-done.36.refs_3_ = bf16[144,512]{1,0:T(8,128)(2,1)S(1)} collective-permute-done((bf16[144,512]{1,0:T(8,128)(2,1)}, bf16[144,512]{1,0:T(8,128)(2,1)S(1)}, u32[]{:S(2)}, u32[]{:S(2)}) %collective-permute-start.36) | collective-permute-done | bytes 147488 | tf_op jit(solution)/shard_map/ppermute | solution.py:273
  (193 shorter events, 81.3 us)
Async XLA Ops:
  7.2 67.9 %all-gather.5.cloned.1.call-start = ((), (), s32[]{:S(2)}) async-start(), calls=%async_computation.4 | async-start | bytes 4718592 | tf_op jit(solution)/shard_map/all_gather | solution.py:1021
  30.4 86.7 %all-gather.7.cloned.1.call-start = ((), (), s32[]{:S(2)}) async-start(), calls=%async_computation.5 | async-start | bytes 4718592 | tf_op jit(solution)/shard_map/all_gather | solution.py:1025
  30.5 41.2 %collective-permute-start.6 = (bf16[3,160,512]{2,1,0:T(8,128)(2,1)S(1)}, bf16[3,160,512]{2,1,0:T(8,128)(2,1)S(1)}, u32[]{:S(2)}, u32[]{:S(2)}) collective-permute-start(bf16[3,160,512]{2,1,0:T(8,128)(2,1)S(1)} %copy-done.8), channel_id=1, source_target_pairs={{0,1},{1,0},{2,3},{3,2},{4,5},{5,4},{6,7},{7,6},{8,9},{9,8},{10,11... | collective-permute-start | bytes 1474568 | tf_op jit(solution)/shard_map/ppermute | solution.py:273
  34.9 33.6 %collective-permute-start.7 = (bf16[3,80,512]{2,1,0:T(8,128)(2,1)S(1)}, bf16[3,80,512]{2,1,0:T(8,128)(2,1)S(1)}, u32[]{:S(2)}, u32[]{:S(2)}) collective-permute-start(bf16[3,80,512]{2,1,0:T(8,128)(2,1)S(1)} %copy-done.19), channel_id=1, source_target_pairs={{0,2},{1,3},{2,0},{3,1},{4,6},{5,7},{6,4},{7,5},{8,10},{9,11},{10,... | collective-permute-start | bytes 737288 | tf_op jit(solution)/shard_map/ppermute | solution.py:273
  35.0 35.5 %collective-permute-start.8 = (bf16[3,80,512]{2,1,0:T(8,128)(2,1)S(1)}, bf16[3,80,512]{2,1,0:T(8,128)(2,1)S(1)}, u32[]{:S(2)}, u32[]{:S(2)}) collective-permute-start(bf16[3,80,512]{2,1,0:T(8,128)(2,1)S(1)} %copy-done.18), channel_id=1, source_target_pairs={{0,3},{1,2},{2,1},{3,0},{4,7},{5,6},{6,5},{7,4},{8,11},{9,10},{10,... | collective-permute-start | bytes 737288 | tf_op jit(solution)/shard_map/ppermute | solution.py:273
  37.4 25.1 %collective-permute-start.11 = (bf16[128,512]{1,0:T(8,128)(2,1)S(1)}, bf16[128,512]{1,0:T(8,128)(2,1)S(1)}, u32[]{:S(2)}, u32[]{:S(2)}) collective-permute-start(bf16[128,512]{1,0:T(8,128)(2,1)S(1)} %copy-done.26), channel_id=1, source_target_pairs={{0,3},{1,2},{2,1},{3,0},{4,7},{5,6},{6,5},{7,4},{8,11},{9,10},{10,... | collective-permute-start | bytes 393224 | tf_op jit(solution)/shard_map/ppermute | solution.py:273
  46.0 22.0 %collective-permute-start.9 = (bf16[128,512]{1,0:T(8,128)(2,1)S(1)}, bf16[128,512]{1,0:T(8,128)(2,1)S(1)}, u32[]{:S(2)}, u32[]{:S(2)}) collective-permute-start(bf16[128,512]{1,0:T(8,128)(2,1)S(1)} %copy-done.26), channel_id=1, source_target_pairs={{0,1},{1,0},{2,3},{3,2},{4,5},{5,4},{6,7},{7,6},{8,9},{9,8},{10,11... | collective-permute-start | bytes 393224 | tf_op jit(solution)/shard_map/ppermute | solution.py:273
  62.5 34.3 %collective-permute-start = (bf16[3,160,512]{2,1,0:T(8,128)(2,1)S(1)}, bf16[3,160,512]{2,1,0:T(8,128)(2,1)S(1)}, u32[]{:S(2)}, u32[]{:S(2)}) collective-permute-start(bf16[3,160,512]{2,1,0:T(8,128)(2,1)S(1)} %copy-done.34), channel_id=1, source_target_pairs={{0,1},{1,0},{2,3},{3,2},{4,5},{5,4},{6,7},{7,6},{8,9},{9,8},{10,11... | collective-permute-start | bytes 1474568 | tf_op jit(solution)/shard_map/ppermute | solution.py:273
  68.0 26.7 %collective-permute-start.1 = (bf16[3,80,512]{2,1,0:T(8,128)(2,1)S(1)}, bf16[3,80,512]{2,1,0:T(8,128)(2,1)S(1)}, u32[]{:S(2)}, u32[]{:S(2)}) collective-permute-start(bf16[3,80,512]{2,1,0:T(8,128)(2,1)S(1)} %copy-done.42), channel_id=1, source_target_pairs={{0,2},{1,3},{2,0},{3,1},{4,6},{5,7},{6,4},{7,5},{8,10},{9,11},{10,... | collective-permute-start | bytes 737288 | tf_op jit(solution)/shard_map/ppermute | solution.py:273
  68.6 28.2 %collective-permute-start.2 = (bf16[3,80,512]{2,1,0:T(8,128)(2,1)S(1)}, bf16[3,80,512]{2,1,0:T(8,128)(2,1)S(1)}, u32[]{:S(2)}, u32[]{:S(2)}) collective-permute-start(bf16[3,80,512]{2,1,0:T(8,128)(2,1)S(1)} %copy-done.41), channel_id=1, source_target_pairs={{0,3},{1,2},{2,1},{3,0},{4,7},{5,6},{6,5},{7,4},{8,11},{9,10},{10,... | collective-permute-start | bytes 737288 | tf_op jit(solution)/shard_map/ppermute | solution.py:273
  70.5 46.5 %collective-permute-start.12 = (bf16[3,160,512]{2,1,0:T(8,128)(2,1)}, bf16[3,160,512]{2,1,0:T(8,128)(2,1)S(1)}, u32[]{:S(2)}, u32[]{:S(2)}) collective-permute-start(bf16[3,160,512]{2,1,0:T(8,128)(2,1)} %get-tuple-element.132), channel_id=1, source_target_pairs={{0,1},{1,0},{2,3},{3,2},{4,5},{5,4},{6,7},{7,6},{8,9},{9,8},{10,11... | collective-permute-start | bytes 1474568 | tf_op jit(solution)/shard_map/ppermute | solution.py:273
  71.6 45.4 %collective-permute-start.13 = (bf16[3,80,512]{2,1,0:T(8,128)(2,1)}, bf16[3,80,512]{2,1,0:T(8,128)(2,1)S(1)}, u32[]{:S(2)}, u32[]{:S(2)}) collective-permute-start(bf16[3,80,512]{2,1,0:T(8,128)(2,1)} %get-tuple-element.133), channel_id=1, source_target_pairs={{0,2},{1,3},{2,0},{3,1},{4,6},{5,7},{6,4},{7,5},{8,10},{9,11},{10,... | collective-permute-start | bytes 737288 | tf_op jit(solution)/shard_map/ppermute | solution.py:273
  75.0 177.9 %reduce-scatter.3.cloned.1.call-start = ((), (), s32[]{:S(2)}) async-start(), calls=%async_computation.2 | async-start | bytes 4718592 | tf_op jit(solution)/shard_map/reduce_scatter | solution.py:1051
  94.7 22.4 %collective-permute-start.14 = (bf16[3,80,512]{2,1,0:T(8,128)(2,1)S(1)}, bf16[3,80,512]{2,1,0:T(8,128)(2,1)S(1)}, u32[]{:S(2)}, u32[]{:S(2)}) collective-permute-start(bf16[3,80,512]{2,1,0:T(8,128)(2,1)S(1)} %copy-done.40), channel_id=1, source_target_pairs={{0,3},{1,2},{2,1},{3,0},{4,7},{5,6},{6,5},{7,4},{8,11},{9,10},{10,... | collective-permute-start | bytes 737288 | tf_op jit(solution)/shard_map/ppermute | solution.py:273
  137.6 40.9 %collective-permute-start.15 = (bf16[3,160,512]{2,1,0:T(8,128)(2,1)}, bf16[3,160,512]{2,1,0:T(8,128)(2,1)S(1)}, u32[]{:S(2)}, u32[]{:S(2)}) collective-permute-start(bf16[3,160,512]{2,1,0:T(8,128)(2,1)} %get-tuple-element.144), channel_id=1, source_target_pairs={{0,1},{1,0},{2,3},{3,2},{4,5},{5,4},{6,7},{7,6},{8,9},{9,8},{10,11... | collective-permute-start | bytes 1474568 | tf_op jit(solution)/shard_map/ppermute | solution.py:273
  138.1 38.7 %collective-permute-start.16 = (bf16[3,80,512]{2,1,0:T(8,128)(2,1)}, bf16[3,80,512]{2,1,0:T(8,128)(2,1)S(1)}, u32[]{:S(2)}, u32[]{:S(2)}) collective-permute-start(bf16[3,80,512]{2,1,0:T(8,128)(2,1)} %get-tuple-element.145), channel_id=1, source_target_pairs={{0,2},{1,3},{2,0},{3,1},{4,6},{5,7},{6,4},{7,5},{8,10},{9,11},{10,... | collective-permute-start | bytes 737288 | tf_op jit(solution)/shard_map/ppermute | solution.py:273
  140.5 37.9 %collective-permute-start.17 = (bf16[3,80,512]{2,1,0:T(8,128)(2,1)}, bf16[3,80,512]{2,1,0:T(8,128)(2,1)S(1)}, u32[]{:S(2)}, u32[]{:S(2)}) collective-permute-start(bf16[3,80,512]{2,1,0:T(8,128)(2,1)} %get-tuple-element.146), channel_id=1, source_target_pairs={{0,3},{1,2},{2,1},{3,0},{4,7},{5,6},{6,5},{7,4},{8,11},{9,10},{10,... | collective-permute-start | bytes 737288 | tf_op jit(solution)/shard_map/ppermute | solution.py:273
  173.8 29.6 %collective-permute-start.19 = (bf16[3,160,512]{2,1,0:T(8,128)(2,1)}, bf16[3,160,512]{2,1,0:T(8,128)(2,1)S(1)}, u32[]{:S(2)}, u32[]{:S(2)}) collective-permute-start(bf16[3,160,512]{2,1,0:T(8,128)(2,1)} %get-tuple-element.157), channel_id=1, source_target_pairs={{0,1},{1,0},{2,3},{3,2},{4,5},{5,4},{6,7},{7,6},{8,9},{9,8},{10,11... | collective-permute-start | bytes 1474568 | tf_op jit(solution)/shard_map/ppermute | solution.py:273
  173.9 29.5 %collective-permute-start.20 = (bf16[3,80,512]{2,1,0:T(8,128)(2,1)}, bf16[3,80,512]{2,1,0:T(8,128)(2,1)S(1)}, u32[]{:S(2)}, u32[]{:S(2)}) collective-permute-start(bf16[3,80,512]{2,1,0:T(8,128)(2,1)} %get-tuple-element.158), channel_id=1, source_target_pairs={{0,2},{1,3},{2,0},{3,1},{4,6},{5,7},{6,4},{7,5},{8,10},{9,11},{10,... | collective-permute-start | bytes 737288 | tf_op jit(solution)/shard_map/ppermute | solution.py:273
  176.8 100.0 %reduce-scatter.5.cloned.1.call-start = ((), (), s32[]{:S(2)}) async-start(), calls=%async_computation.3 | async-start | bytes 655360 | tf_op jit(solution)/shard_map/reduce_scatter | solution.py:1073
  176.9 26.6 %collective-permute-start.21 = (bf16[3,80,512]{2,1,0:T(8,128)(2,1)S(1)}, bf16[3,80,512]{2,1,0:T(8,128)(2,1)S(1)}, u32[]{:S(2)}, u32[]{:S(2)}) collective-permute-start(bf16[3,80,512]{2,1,0:T(8,128)(2,1)S(1)} %copy-done.47), channel_id=1, source_target_pairs={{0,3},{1,2},{2,1},{3,0},{4,7},{5,6},{6,5},{7,4},{8,11},{9,10},{10,... | collective-permute-start | bytes 737288 | tf_op jit(solution)/shard_map/ppermute | solution.py:273
  214.6 42.2 %collective-permute-start.25 = (bf16[3,160,512]{2,1,0:T(8,128)(2,1)}, bf16[3,160,512]{2,1,0:T(8,128)(2,1)S(1)}, u32[]{:S(2)}, u32[]{:S(2)}) collective-permute-start(bf16[3,160,512]{2,1,0:T(8,128)(2,1)} %get-tuple-element.182), channel_id=1, source_target_pairs={{0,1},{1,0},{2,3},{3,2},{4,5},{5,4},{6,7},{7,6},{8,9},{9,8},{10,11... | collective-permute-start | bytes 1474568 | tf_op jit(solution)/shard_map/ppermute | solution.py:273
  214.7 38.2 %collective-permute-start.26 = (bf16[3,80,512]{2,1,0:T(8,128)(2,1)}, bf16[3,80,512]{2,1,0:T(8,128)(2,1)S(1)}, u32[]{:S(2)}, u32[]{:S(2)}) collective-permute-start(bf16[3,80,512]{2,1,0:T(8,128)(2,1)} %get-tuple-element.183), channel_id=1, source_target_pairs={{0,2},{1,3},{2,0},{3,1},{4,6},{5,7},{6,4},{7,5},{8,10},{9,11},{10,... | collective-permute-start | bytes 737288 | tf_op jit(solution)/shard_map/ppermute | solution.py:273
  236.6 23.4 %collective-permute-start.29 = (bf16[3,160,512]{2,1,0:T(8,128)(2,1)}, bf16[3,160,512]{2,1,0:T(8,128)(2,1)S(1)}, u32[]{:S(2)}, u32[]{:S(2)}) collective-permute-start(bf16[3,160,512]{2,1,0:T(8,128)(2,1)} %get-tuple-element.186), channel_id=1, source_target_pairs={{0,1},{1,0},{2,3},{3,2},{4,5},{5,4},{6,7},{7,6},{8,9},{9,8},{10,11... | collective-permute-start | bytes 1474568 | tf_op jit(solution)/shard_map/ppermute | solution.py:273
  (68 other events, 593.1 us)
Sparse Core Ops, SparseCore 0:
  30.5 38.1 all-gather.4
  75.1 36.2 all-gather.6
  176.9 52.8 reduce-scatter.2
  253.1 19.3 reduce-scatter.4

commit v3 on v2

--- a/solution.py
+++ b/solution.py
@@ -642,24 +642,32 @@
     return h * cdf, cdf + h * e
 
 
-def mlp_clip(x, gain, bias, w_ref, c_ref, gb_ref, u_ref, dh_ref, slope_ref, y_ref, send_refs, grad_of):
+def mlp_clip(x, gain, bias, w_ref, c_ref, gb_ref, u_ref, dh_ref, slope_ref, y_ref, send_refs, grad_of, early=False):
     tiles = w_ref.shape[1]
     unit, scale = normalize(x)
     c_ref[...] = (unit * gain + bias).astype(BF16)
+    dy = grad_of(None) if early else None
+    hidden = [dot(c_ref[...], hidden_weight(w_ref, j, 0)) for j in range(tiles)] if early else None
     for j in range(tiles):
-        active, slope = gelu_parts(dot(c_ref[...], hidden_weight(w_ref, j, 0)))
+        if early:
+            du = dot_nt(gb_ref[...], hidden_weight(w_ref, j, 1))
+            active, slope = gelu_parts(hidden[j])
+            dh_ref[j] = (du * slope).astype(BF16)
+        else:
+            active, slope = gelu_parts(dot(c_ref[...], hidden_weight(w_ref, j, 0)))
+            slope_ref[j] = slope.astype(BF16)
         u_ref[j] = active.astype(BF16)
-        slope_ref[j] = slope.astype(BF16)
     y = x + dot(
         jnp.concatenate([u_ref[j] for j in range(tiles)], axis=1),
         jnp.concatenate([hidden_weight(w_ref, j, 1) for j in range(tiles)], axis=0),
     )
     y_ref[...] = y.astype(BF16)
     write_sends(y_ref[...], send_refs)
-    dy = grad_of(y)
-    for j in range(tiles):
-        du = dot_nt(gb_ref[...], hidden_weight(w_ref, j, 1))
-        dh_ref[j] = (du * slope_ref[j].astype(F32)).astype(BF16)
+    if not early:
+        dy = grad_of(y)
+        for j in range(tiles):
+            du = dot_nt(gb_ref[...], hidden_weight(w_ref, j, 1))
+            dh_ref[j] = (du * slope_ref[j].astype(F32)).astype(BF16)
     dc = dot_nt(
         jnp.concatenate([dh_ref[j] for j in range(tiles)], axis=1),
         jnp.concatenate([hidden_weight(w_ref, j, 0) for j in range(tiles)], axis=1),
@@ -683,7 +691,7 @@
         gb_ref[...] = grad_ref[...]
     dx, dg, db = mlp_clip(
         x_ref[0], gain_ref[...], bias_ref[...], w_ref, c_ref.at[0], gb_ref.at[0], u_ref.at[:, 0], dh_ref.at[:, 0], slope_ref,
-        y_ref.at[0], send_refs, lambda y: gb_ref[0].astype(F32),
+        y_ref.at[0], send_refs, lambda y: gb_ref[0].astype(F32), True,
     )
     dx_ref[0] = dx
     dg_ref[...] += dg

time: 312 us -> 311 us (level)
  transfers between devices with their start and end apart: 42 -> 42, of which waited for: 7 -> 7; matrix products, arithmetic and copies ran while one was open for 1% -> 1% of each run, Pallas kernels for 53% -> 52%
where the time goes in v3:
time: 311 us; the launch traced here: 308 us
  Pallas kernels  187 us (60%)
  starting transfers between devices  59.9 us (19%)
  waiting for transfers between devices  31.1 us (10%)
  between operations  16 us (5%)
  local copies, waits for them, and re-layouts  11.4 us (4%)
    pallas_call x24, Pallas kernels, run(): pl.pallas_call(body, grid=grid, in_specs=list(in_specs) + [HBM] * extra,...  187 us
    ppermute x38, starting transfers between devices, swap(): lax.ppermute(x, axis, [(i, i ^ way) for i in range(lax.axis_size(axis))])  59.2 us
    ppermute x38, waiting for transfers between devices, swap(): lax.ppermute(x, axis, [(i, i ^ way) for i in range(lax.axis_size(axis))])  31 us
    unnamed x100, local copies, waits for them, and re-layouts  10 us
  transfers between devices with their start and end apart: 42, of which 7 were waited for; matrix products, arithmetic and copies ran while one was open for 1% of the time, Pallas kernels for 52%

profile of v3, /device:TPU:0, one launch (start us, length us, event | category | flops | bytes accessed | tf_op | source)
XLA Modules:
  0.0 308.0 jit_solution(13722392278230730880)
XLA Ops:
  10.1 3.0 collective-permute-start.3
  17.0 3.3 %shard_map.352 = (bf16[3,160,512]{2,1,0:T(8,128)(2,1)}, bf16[3,80,512]{2,1,0:T(8,128)(2,1)}, bf16[3,80,512]{2,1,0:T(8,128)(2,1)}) custom-call(s32[2]{0:T(128)} %pad_add_fusion.refs_0_.refs_2_, s32[3]{0:T(128)} %refs_1_.17, bf16[3,320,512]{2,1,0:T(8,128)(2,1)} %bitcast.44, bf16[128,512]{1,0:T(8,128)(2,1)} %get-tuple-element.112.refs_3_.refs_1_), custom_call_target="tpu_custom_call" | custom-call | flops 25000000 | tf_op jit(solution)/shard_map/pallas_call | solution.py:67
  20.4 3.3 %shard_map.353 = (bf16[3,160,512]{2,1,0:T(8,128)(2,1)}, bf16[3,80,512]{2,1,0:T(8,128)(2,1)}, bf16[3,80,512]{2,1,0:T(8,128)(2,1)}) custom-call(s32[2]{0:T(128)} %pad_add_fusion.refs_0_.refs_2_, s32[3]{0:T(128)} %refs_1_.19, bf16[3,320,512]{2,1,0:T(8,128)(2,1)} %bitcast.42, bf16[3,160,512]{2,1,0:T(8,128)(2,1)} %get-tuple-element.113.refs_3_, ...), custom_call_target="tpu_custom_call" | custom-call | flops 25000000 | tf_op jit(solution)/shard_map/pallas_call | solution.py:67
  23.7 4.0 %shard_map.354 = (bf16[3,320,512]{2,1,0:T(8,128)(2,1)}, bf16[3,160,512]{2,1,0:T(8,128)(2,1)}, bf16[3,80,512]{2,1,0:T(8,128)(2,1)}, bf16[3,80,512]{2,1,0:T(8,128)(2,1)}) custom-call(s32[2]{0:T(128)} %pad_add_fusion.refs_0_.refs_2_, s32[3]{0:T(128)} %refs_1_.17, s32[3]{0:T(128)} %refs_2_.3, f32[1]{0:T(128)S(6)} %div.3.refs_3_, bf16[3,320,512]{2,1,0:T(8,128)(2,1)} %bitcast.58, ...), custom_call_target="tpu_custom_call" | custom-call | flops 10000000000 | tf_op jit(solution)/shard_map/pallas_call | solution.py:67
  31.4 3.5 %collective-permute-start.10 = (bf16[128,512]{1,0:T(8,128)(2,1)S(1)}, bf16[128,512]{1,0:T(8,128)(2,1)S(1)}, u32[]{:S(2)}, u32[]{:S(2)}) collective-permute-start(bf16[128,512]{1,0:T(8,128)(2,1)S(1)} %copy-done.26), channel_id=1, source_target_pairs={{0,2},{1,3},{2,0},{3,1},{4,6},{5,7},{6,4},{7,5},{8,10},{9,11},{10,... | collective-permute-start | bytes 393224 | tf_op jit(solution)/shard_map/ppermute | solution.py:273
  38.8 7.1 %collective-permute-done.10.refs_3_ = bf16[128,512]{1,0:T(8,128)(2,1)S(1)} collective-permute-done((bf16[128,512]{1,0:T(8,128)(2,1)S(1)}, bf16[128,512]{1,0:T(8,128)(2,1)S(1)}, u32[]{:S(2)}, u32[]{:S(2)}) %collective-permute-start.10) | collective-permute-done | bytes 131104 | tf_op jit(solution)/shard_map/ppermute | solution.py:273
  46.0 4.0 %collective-permute-start.9 = (bf16[128,512]{1,0:T(8,128)(2,1)S(1)}, bf16[128,512]{1,0:T(8,128)(2,1)S(1)}, u32[]{:S(2)}, u32[]{:S(2)}) collective-permute-start(bf16[128,512]{1,0:T(8,128)(2,1)S(1)} %copy-done.26), channel_id=1, source_target_pairs={{0,1},{1,0},{2,3},{3,2},{4,5},{5,4},{6,7},{7,6},{8,9},{9,8},{10,11... | collective-permute-start | bytes 393224 | tf_op jit(solution)/shard_map/ppermute | solution.py:273
  50.5 11.9 %collective-permute-done.11.refs_4_ = bf16[128,512]{1,0:T(8,128)(2,1)S(1)} collective-permute-done((bf16[128,512]{1,0:T(8,128)(2,1)S(1)}, bf16[128,512]{1,0:T(8,128)(2,1)S(1)}, u32[]{:S(2)}, u32[]{:S(2)}) %collective-permute-start.11) | collective-permute-done | bytes 131104 | tf_op jit(solution)/shard_map/ppermute | solution.py:273
  62.5 5.5 %collective-permute-start = (bf16[3,160,512]{2,1,0:T(8,128)(2,1)S(1)}, bf16[3,160,512]{2,1,0:T(8,128)(2,1)S(1)}, u32[]{:S(2)}, u32[]{:S(2)}) collective-permute-start(bf16[3,160,512]{2,1,0:T(8,128)(2,1)S(1)} %copy-done.34), channel_id=1, source_target_pairs={{0,1},{1,0},{2,3},{3,2},{4,5},{5,4},{6,7},{7,6},{8,9},{9,8},{10,11... | collective-permute-start | bytes 1474568 | tf_op jit(solution)/shard_map/ppermute | solution.py:273
  75.6 8.8 %shard_map.357 = (f32[6,320,512]{2,1,0:T(8,128)}, bf16[6,320,1536]{2,1,0:T(8,128)(2,1)}, bf16[6,10,64,256]{3,2,1,0:T(8,128)(2,1)}, bf16[6,320,512]{2,1,0:T(8,128)(2,1)}, bf16[6,320,512]{2,1,0:T(8,128)(2,1)}) custom-call(s32[2]{0:T(128)} %pad_add_fusion.refs_0_.refs_2_, s32[3]{0:T(128)} %refs_1_.17, bf16[3,320,512]{2,1,0:T(8,128)(2,1)} %bitcast.45, ...), custom_call_target="tpu_custom_call" | custom-call | flops 24999999488 | tf_op jit(solution)/shard_map/pallas_call | solution.py:67
  84.4 10.2 %shard_map.358 = (f32[6,320,512]{2,1,0:T(8,128)}, bf16[6,320,1536]{2,1,0:T(8,128)(2,1)}, f32[6,320,128]{2,1,0:T(8,128)}, bf16[6,320,512]{2,1,0:T(8,128)(2,1)}) custom-call(f32[6,320,512]{2,1,0:T(8,128)} %get-tuple-element.121.refs_0_.refs_10_, f32[1,512]{1,0:T(1,128)} %bitcast.67, f32[1,512]{1,0:T(1,128)} %bitcast.70, bf16[8,4,128,512]{3,2,1,0:T(8,128)(2,1)} %bitcast.50), custom_call_target="tpu_custom_call" | custom-call | flops 24999999488 | tf_op jit(solution)/shard_map/pallas_call | solution.py:67
  97.6 8.9 %shard_map.359 = (f32[6,320,512]{2,1,0:T(8,128)}, bf16[6,320,1536]{2,1,0:T(8,128)(2,1)}, bf16[6,10,64,256]{3,2,1,0:T(8,128)(2,1)}, bf16[6,320,512]{2,1,0:T(8,128)(2,1)}, bf16[6,320,512]{2,1,0:T(8,128)(2,1)}) custom-call(s32[2]{0:T(128)} %pad_add_fusion.refs_0_.refs_2_, ...), custom_call_target="tpu_custom_call", output_to_operand_aliasing={{0}: (10, {}), {1}: (11, {}), {2}: (12, {}), {3}: (13, {}),... | custom-call | flops 24999999488 | tf_op jit(solution)/shard_map/pallas_call | solution.py:67
  106.5 10.5 %shard_map.360 = (f32[6,320,512]{2,1,0:T(8,128)}, bf16[6,320,1536]{2,1,0:T(8,128)(2,1)}, f32[6,320,128]{2,1,0:T(8,128)}, bf16[6,320,512]{2,1,0:T(8,128)(2,1)}) custom-call(f32[6,320,512]{2,1,0:T(8,128)} %get-tuple-element.127.refs_0_.refs_2_, f32[1,512]{1,0:T(1,128)} %bitcast.68, ...), custom_call_target="tpu_custom_call", output_to_operand_aliasing={{0}: (4, {}), {1}: (5, {}), {2}: (6, {}), {3}: (7, {})} | custom-call | flops 24999999488 | tf_op jit(solution)/shard_map/pallas_call | solution.py:67
  118.0 19.2 %shard_map.361 = (bf16[6,320,512]{2,1,0:T(8,128)(2,1)}, f32[6,320,512]{2,1,0:T(8,128)}, bf16[3,320,512]{2,1,0:T(8,128)(2,1)}, bf16[3,320,512]{2,1,0:T(8,128)(2,1...) custom-call(s32[2]{0:T(128)} %pad_add_fusion.refs_0_.refs_2_, ...), custom_call_target="tpu_custom_call" | custom-call | flops 49999998976 | tf_op jit(solution)/shard_map/pallas_call | solution.py:67
  141.6 31.8 %shard_map.362 = (bf16[6,320,512]{2,1,0:T(8,128)(2,1)}, f32[6,320,512]{2,1,0:T(8,128)}, bf16[8,4,128,512]{3,2,1,0:T(8,128)(2,1)}, f32[8,512]{1,0:T(8,128)}, f32[...) custom-call(f32[3]{0:T(128)} %add_convert_fusion.refs_0_, ...), custom_call_target="tpu_custom_call", output_to_operand_aliasing={{0}: (14, {}), {1}: (15, {})} | custom-call | flops 74999996416 | tf_op jit(solution)/shard_map/pallas_call | solution.py:67
  178.9 24.0 %shard_map.363 = (f32[6,320,512]{2,1,0:T(8,128)}, f32[8,512]{1,0:T(8,128)}, f32[8,512]{1,0:T(8,128)}, bf16[4,4,64,512]{3,2,1,0:T(8,128)(2,1)}, bf16[4,4,64,512]{3,2,1,0:T(8,128)(2,1)}) custom-call(s32[2]{0:T(128)} %pad_add_fusion.refs_0_.refs_2_, f32[6,320,512]{2,1,0:T(8,128)} %get-tuple-element.147.refs_1_, ...), custom_call_target="tpu_custom_call" | custom-call | flops 65000001536 | tf_op jit(solution)/shard_map/pallas_call | solution.py:67
  204.1 10.2 %shard_map.364 = (bf16[6,320,1536]{2,1,0:T(8,128)(2,1)}, bf16[6,320,512]{2,1,0:T(8,128)(2,1)}, bf16[6,320,512]{2,1,0:T(8,128)(2,1)}, bf16[3,320,512]{2,1,0:T(8,1...) custom-call(f32[6,320,512]{2,1,0:T(8,128)} %get-tuple-element.151.re, ...), custom_call_target="tpu_custom_call" | custom-call | flops 24999999488 | tf_op jit(solution)/shard_map/pallas_call | solution.py:67
  224.0 10.3 %shard_map.366 = (bf16[6,320,1536]{2,1,0:T(8,128)(2,1)}, bf16[6,320,512]{2,1,0:T(8,128)(2,1)}, bf16[6,320,512]{2,1,0:T(8,128)(2,1)}, bf16[3,320,512]{2,1,0:T(8,1...) custom-call(f32[6,320,512]{2,1,0:T(8,128)} %get-tuple-element.151.re, ...), custom_call_target="tpu_custom_call", output_to_operand_aliasing={{0}: (8, {}), {1}: (9, {}), {2}: (10, {})} | custom-call | flops 24999999488 | tf_op jit(solution)/shard_map/pallas_call | solution.py:67
  241.0 11.5 %shard_map.367 = (bf16[4,4,80,512]{3,2,1,0:T(8,128)(2,1)}, bf16[4,4,80,512]{3,2,1,0:T(8,128)(2,1)}) custom-call(s32[2]{0:T(128)} %pad_add_fusion.refs_0_.refs_2_, bf16[1920,512]{1,0:T(8,128)(2,1)} %bitcast.89, bf16[1920,1536]{1,0:T(8,128)(2,1)} %bitcast.87, bf16[1920,512]{1,0:T(8,128)(2,1)} %bitcast.88, bf16[1920,512]{1,0:T(8,128)(2,1)} %bitcast.90, ...), custom_call_target="tpu_custom_call" | custom-call | flops 15000000512 | tf_op jit(solution)/shard_map/pallas_call | solution.py:67
  252.7 3.7 %shard_map.368.refs_5_ = bf16[3,320,512]{2,1,0:T(8,128)(2,1)} custom-call(s32[2]{0:T(128)} %pad_add_fusion.refs_0_.refs_2_, s32[3]{0:T(128)} %refs_1_.17, bf16[6,320,512]{2,1,0:T(8,128)(2,1)} %get-tuple-element.143.refs_2_, bf16[3,160,512]{2,1,0:T(8,128)(2,1)} %copy-done.33, bf16[3,80,512]{2,1,0:T(8,128)(2,1)} %copy-done.37, bf16[3,80,512]{2,1,0:T(8,128)(2,1)} %copy-done.38, ...), custom_call_target="tpu_custom_call" | custom-call | flops 15000000512 | tf_op jit(solution)/shard_map/pallas_call | solution.py:67
  269.0 3.7 %shard_map.371.refs_9_ = bf16[3,320,512]{2,1,0:T(8,128)(2,1)} custom-call(s32[2]{0:T(128)} %pad_add_fusion.refs_0_.refs_2_, s32[3]{0:T(128)} %refs_1_.19, bf16[6,320,512]{2,1,0:T(8,128)(2,1)} %get-tuple-element.143.refs_2_, bf16[3,160,512]{2,1,0:T(8,128)(2,1)} %copy-done.7, bf16[3,80,512]{2,1,0:T(8,128)(2,1)} %copy-done.16, bf16[3,80,512]{2,1,0:T(8,128)(2,1)} %copy-done.17, ...), custom_call_target="tpu_custom_call" | custom-call | flops 25000000 | tf_op jit(solution)/shard_map/pallas_call | solution.py:67
  272.7 3.7 %shard_map.370.refs_8_ = bf16[3,320,512]{2,1,0:T(8,128)(2,1)} custom-call(s32[2]{0:T(128)} %pad_add_fusion.refs_0_.refs_2_, s32[3]{0:T(128)} %refs_1_.17, bf16[3,320,512]{2,1,0:T(8,128)(2,1)} %get-tuple-element.160.refs_2_, bf16[3,160,512]{2,1,0:T(8,128)(2,1)} %copy-done, bf16[3,80,512]{2,1,0:T(8,128)(2,1)} %copy-done.4, bf16[3,80,512]{2,1,0:T(8,128)(2,1)} %copy-done.6, ...), custom_call_target="tpu_custom_call" | custom-call | flops 25000000 | tf_op jit(solution)/shard_map/pallas_call | solution.py:67
  289.3 3.7 %shard_map.373 = bf16[3,320,512]{2,1,0:T(8,128)(2,1)} custom-call(s32[2]{0:T(128)} %pad_add_fusion.refs_0_.refs_2_, s32[3]{0:T(128)} %refs_1_.19, bf16[3,320,512]{2,1,0:T(8,128)(2,1)} %get-tuple-element.177.refs_17_.refs_2_, bf16[3,160,512]{2,1,0:T(8,128)(2,1)} %copy-done.1, bf16[3,80,512]{2,1,0:T(8,128)(2,1)} %copy-done.5, bf16[3,80,512]{2,1,0:T(8,128)(2,1)} %copy-done.20, ...), custom_call_target="tpu_custom_call" | custom-call | flops 25000000 | tf_op jit(solution)/shard_map/pallas_call | solution.py:67
  293.8 4.2 %collective-permute-done.36.refs_3_ = bf16[144,512]{1,0:T(8,128)(2,1)S(1)} collective-permute-done((bf16[144,512]{1,0:T(8,128)(2,1)}, bf16[144,512]{1,0:T(8,128)(2,1)S(1)}, u32[]{:S(2)}, u32[]{:S(2)}) %collective-permute-start.36) | collective-permute-done | bytes 147488 | tf_op jit(solution)/shard_map/ppermute | solution.py:273
  (193 shorter events, 81.8 us)
Async XLA Ops:
  7.2 68.4 %all-gather.5.cloned.1.call-start = ((), (), s32[]{:S(2)}) async-start(), calls=%async_computation.4 | async-start | bytes 4718592 | tf_op jit(solution)/shard_map/all_gather | solution.py:1029
  30.4 86.7 %all-gather.7.cloned.1.call-start = ((), (), s32[]{:S(2)}) async-start(), calls=%async_computation.5 | async-start | bytes 4718592 | tf_op jit(solution)/shard_map/all_gather | solution.py:1033
  30.5 41.2 %collective-permute-start.6 = (bf16[3,160,512]{2,1,0:T(8,128)(2,1)S(1)}, bf16[3,160,512]{2,1,0:T(8,128)(2,1)S(1)}, u32[]{:S(2)}, u32[]{:S(2)}) collective-permute-start(bf16[3,160,512]{2,1,0:T(8,128)(2,1)S(1)} %copy-done.8), channel_id=1, source_target_pairs={{0,1},{1,0},{2,3},{3,2},{4,5},{5,4},{6,7},{7,6},{8,9},{9,8},{10,11... | collective-permute-start | bytes 1474568 | tf_op jit(solution)/shard_map/ppermute | solution.py:273
  34.9 33.6 %collective-permute-start.7 = (bf16[3,80,512]{2,1,0:T(8,128)(2,1)S(1)}, bf16[3,80,512]{2,1,0:T(8,128)(2,1)S(1)}, u32[]{:S(2)}, u32[]{:S(2)}) collective-permute-start(bf16[3,80,512]{2,1,0:T(8,128)(2,1)S(1)} %copy-done.19), channel_id=1, source_target_pairs={{0,2},{1,3},{2,0},{3,1},{4,6},{5,7},{6,4},{7,5},{8,10},{9,11},{10,... | collective-permute-start | bytes 737288 | tf_op jit(solution)/shard_map/ppermute | solution.py:273
  35.0 35.5 %collective-permute-start.8 = (bf16[3,80,512]{2,1,0:T(8,128)(2,1)S(1)}, bf16[3,80,512]{2,1,0:T(8,128)(2,1)S(1)}, u32[]{:S(2)}, u32[]{:S(2)}) collective-permute-start(bf16[3,80,512]{2,1,0:T(8,128)(2,1)S(1)} %copy-done.18), channel_id=1, source_target_pairs={{0,3},{1,2},{2,1},{3,0},{4,7},{5,6},{6,5},{7,4},{8,11},{9,10},{10,... | collective-permute-start | bytes 737288 | tf_op jit(solution)/shard_map/ppermute | solution.py:273
  37.4 25.1 %collective-permute-start.11 = (bf16[128,512]{1,0:T(8,128)(2,1)S(1)}, bf16[128,512]{1,0:T(8,128)(2,1)S(1)}, u32[]{:S(2)}, u32[]{:S(2)}) collective-permute-start(bf16[128,512]{1,0:T(8,128)(2,1)S(1)} %copy-done.26), channel_id=1, source_target_pairs={{0,3},{1,2},{2,1},{3,0},{4,7},{5,6},{6,5},{7,4},{8,11},{9,10},{10,... | collective-permute-start | bytes 393224 | tf_op jit(solution)/shard_map/ppermute | solution.py:273
  62.5 34.3 %collective-permute-start = (bf16[3,160,512]{2,1,0:T(8,128)(2,1)S(1)}, bf16[3,160,512]{2,1,0:T(8,128)(2,1)S(1)}, u32[]{:S(2)}, u32[]{:S(2)}) collective-permute-start(bf16[3,160,512]{2,1,0:T(8,128)(2,1)S(1)} %copy-done.34), channel_id=1, source_target_pairs={{0,1},{1,0},{2,3},{3,2},{4,5},{5,4},{6,7},{7,6},{8,9},{9,8},{10,11... | collective-permute-start | bytes 1474568 | tf_op jit(solution)/shard_map/ppermute | solution.py:273
  68.0 26.7 %collective-permute-start.1 = (bf16[3,80,512]{2,1,0:T(8,128)(2,1)S(1)}, bf16[3,80,512]{2,1,0:T(8,128)(2,1)S(1)}, u32[]{:S(2)}, u32[]{:S(2)}) collective-permute-start(bf16[3,80,512]{2,1,0:T(8,128)(2,1)S(1)} %copy-done.42), channel_id=1, source_target_pairs={{0,2},{1,3},{2,0},{3,1},{4,6},{5,7},{6,4},{7,5},{8,10},{9,11},{10,... | collective-permute-start | bytes 737288 | tf_op jit(solution)/shard_map/ppermute | solution.py:273
  68.6 28.2 %collective-permute-start.2 = (bf16[3,80,512]{2,1,0:T(8,128)(2,1)S(1)}, bf16[3,80,512]{2,1,0:T(8,128)(2,1)S(1)}, u32[]{:S(2)}, u32[]{:S(2)}) collective-permute-start(bf16[3,80,512]{2,1,0:T(8,128)(2,1)S(1)} %copy-done.41), channel_id=1, source_target_pairs={{0,3},{1,2},{2,1},{3,0},{4,7},{5,6},{6,5},{7,4},{8,11},{9,10},{10,... | collective-permute-start | bytes 737288 | tf_op jit(solution)/shard_map/ppermute | solution.py:273
  70.5 46.5 %collective-permute-start.12 = (bf16[3,160,512]{2,1,0:T(8,128)(2,1)}, bf16[3,160,512]{2,1,0:T(8,128)(2,1)S(1)}, u32[]{:S(2)}, u32[]{:S(2)}) collective-permute-start(bf16[3,160,512]{2,1,0:T(8,128)(2,1)} %get-tuple-element.132), channel_id=1, source_target_pairs={{0,1},{1,0},{2,3},{3,2},{4,5},{5,4},{6,7},{7,6},{8,9},{9,8},{10,11... | collective-permute-start | bytes 1474568 | tf_op jit(solution)/shard_map/ppermute | solution.py:273
  71.6 45.4 %collective-permute-start.13 = (bf16[3,80,512]{2,1,0:T(8,128)(2,1)}, bf16[3,80,512]{2,1,0:T(8,128)(2,1)S(1)}, u32[]{:S(2)}, u32[]{:S(2)}) collective-permute-start(bf16[3,80,512]{2,1,0:T(8,128)(2,1)} %get-tuple-element.133), channel_id=1, source_target_pairs={{0,2},{1,3},{2,0},{3,1},{4,6},{5,7},{6,4},{7,5},{8,10},{9,11},{10,... | collective-permute-start | bytes 737288 | tf_op jit(solution)/shard_map/ppermute | solution.py:273
  75.0 177.5 %reduce-scatter.3.cloned.1.call-start = ((), (), s32[]{:S(2)}) async-start(), calls=%async_computation.2 | async-start | bytes 4718592 | tf_op jit(solution)/shard_map/reduce_scatter | solution.py:1059
  94.7 22.4 %collective-permute-start.14 = (bf16[3,80,512]{2,1,0:T(8,128)(2,1)S(1)}, bf16[3,80,512]{2,1,0:T(8,128)(2,1)S(1)}, u32[]{:S(2)}, u32[]{:S(2)}) collective-permute-start(bf16[3,80,512]{2,1,0:T(8,128)(2,1)S(1)} %copy-done.40), channel_id=1, source_target_pairs={{0,3},{1,2},{2,1},{3,0},{4,7},{5,6},{6,5},{7,4},{8,11},{9,10},{10,... | collective-permute-start | bytes 737288 | tf_op jit(solution)/shard_map/ppermute | solution.py:273
  137.2 40.9 %collective-permute-start.15 = (bf16[3,160,512]{2,1,0:T(8,128)(2,1)}, bf16[3,160,512]{2,1,0:T(8,128)(2,1)S(1)}, u32[]{:S(2)}, u32[]{:S(2)}) collective-permute-start(bf16[3,160,512]{2,1,0:T(8,128)(2,1)} %get-tuple-element.144), channel_id=1, source_target_pairs={{0,1},{1,0},{2,3},{3,2},{4,5},{5,4},{6,7},{7,6},{8,9},{9,8},{10,11... | collective-permute-start | bytes 1474568 | tf_op jit(solution)/shard_map/ppermute | solution.py:273
  137.8 38.7 %collective-permute-start.16 = (bf16[3,80,512]{2,1,0:T(8,128)(2,1)}, bf16[3,80,512]{2,1,0:T(8,128)(2,1)S(1)}, u32[]{:S(2)}, u32[]{:S(2)}) collective-permute-start(bf16[3,80,512]{2,1,0:T(8,128)(2,1)} %get-tuple-element.145), channel_id=1, source_target_pairs={{0,2},{1,3},{2,0},{3,1},{4,6},{5,7},{6,4},{7,5},{8,10},{9,11},{10,... | collective-permute-start | bytes 737288 | tf_op jit(solution)/shard_map/ppermute | solution.py:273
  140.2 37.9 %collective-permute-start.17 = (bf16[3,80,512]{2,1,0:T(8,128)(2,1)}, bf16[3,80,512]{2,1,0:T(8,128)(2,1)S(1)}, u32[]{:S(2)}, u32[]{:S(2)}) collective-permute-start(bf16[3,80,512]{2,1,0:T(8,128)(2,1)} %get-tuple-element.146), channel_id=1, source_target_pairs={{0,3},{1,2},{2,1},{3,0},{4,7},{5,6},{6,5},{7,4},{8,11},{9,10},{10,... | collective-permute-start | bytes 737288 | tf_op jit(solution)/shard_map/ppermute | solution.py:273
  173.5 29.6 %collective-permute-start.19 = (bf16[3,160,512]{2,1,0:T(8,128)(2,1)}, bf16[3,160,512]{2,1,0:T(8,128)(2,1)S(1)}, u32[]{:S(2)}, u32[]{:S(2)}) collective-permute-start(bf16[3,160,512]{2,1,0:T(8,128)(2,1)} %get-tuple-element.157), channel_id=1, source_target_pairs={{0,1},{1,0},{2,3},{3,2},{4,5},{5,4},{6,7},{7,6},{8,9},{9,8},{10,11... | collective-permute-start | bytes 1474568 | tf_op jit(solution)/shard_map/ppermute | solution.py:273
  173.5 29.5 %collective-permute-start.20 = (bf16[3,80,512]{2,1,0:T(8,128)(2,1)}, bf16[3,80,512]{2,1,0:T(8,128)(2,1)S(1)}, u32[]{:S(2)}, u32[]{:S(2)}) collective-permute-start(bf16[3,80,512]{2,1,0:T(8,128)(2,1)} %get-tuple-element.158), channel_id=1, source_target_pairs={{0,2},{1,3},{2,0},{3,1},{4,6},{5,7},{6,4},{7,5},{8,10},{9,11},{10,... | collective-permute-start | bytes 737288 | tf_op jit(solution)/shard_map/ppermute | solution.py:273
  176.4 100.0 %reduce-scatter.5.cloned.1.call-start = ((), (), s32[]{:S(2)}) async-start(), calls=%async_computation.3 | async-start | bytes 655360 | tf_op jit(solution)/shard_map/reduce_scatter | solution.py:1081
  176.5 26.6 %collective-permute-start.21 = (bf16[3,80,512]{2,1,0:T(8,128)(2,1)S(1)}, bf16[3,80,512]{2,1,0:T(8,128)(2,1)S(1)}, u32[]{:S(2)}, u32[]{:S(2)}) collective-permute-start(bf16[3,80,512]{2,1,0:T(8,128)(2,1)S(1)} %copy-done.47), channel_id=1, source_target_pairs={{0,3},{1,2},{2,1},{3,0},{4,7},{5,6},{6,5},{7,4},{8,11},{9,10},{10,... | collective-permute-start | bytes 737288 | tf_op jit(solution)/shard_map/ppermute | solution.py:273
  214.2 42.2 %collective-permute-start.25 = (bf16[3,160,512]{2,1,0:T(8,128)(2,1)}, bf16[3,160,512]{2,1,0:T(8,128)(2,1)S(1)}, u32[]{:S(2)}, u32[]{:S(2)}) collective-permute-start(bf16[3,160,512]{2,1,0:T(8,128)(2,1)} %get-tuple-element.182), channel_id=1, source_target_pairs={{0,1},{1,0},{2,3},{3,2},{4,5},{5,4},{6,7},{7,6},{8,9},{9,8},{10,11... | collective-permute-start | bytes 1474568 | tf_op jit(solution)/shard_map/ppermute | solution.py:273
  214.3 38.2 %collective-permute-start.26 = (bf16[3,80,512]{2,1,0:T(8,128)(2,1)}, bf16[3,80,512]{2,1,0:T(8,128)(2,1)S(1)}, u32[]{:S(2)}, u32[]{:S(2)}) collective-permute-start(bf16[3,80,512]{2,1,0:T(8,128)(2,1)} %get-tuple-element.183), channel_id=1, source_target_pairs={{0,2},{1,3},{2,0},{3,1},{4,6},{5,7},{6,4},{7,5},{8,10},{9,11},{10,... | collective-permute-start | bytes 737288 | tf_op jit(solution)/shard_map/ppermute | solution.py:273
  234.4 22.0 %collective-permute-start.27 = (bf16[3,80,512]{2,1,0:T(8,128)(2,1)S(1)}, bf16[3,80,512]{2,1,0:T(8,128)(2,1)S(1)}, u32[]{:S(2)}, u32[]{:S(2)}) collective-permute-start(bf16[3,80,512]{2,1,0:T(8,128)(2,1)S(1)} %copy-done.43), channel_id=1, source_target_pairs={{0,3},{1,2},{2,1},{3,0},{4,7},{5,6},{6,5},{7,4},{8,11},{9,10},{10,... | collective-permute-start | bytes 737288 | tf_op jit(solution)/shard_map/ppermute | solution.py:273
  236.2 23.4 %collective-permute-start.29 = (bf16[3,160,512]{2,1,0:T(8,128)(2,1)}, bf16[3,160,512]{2,1,0:T(8,128)(2,1)S(1)}, u32[]{:S(2)}, u32[]{:S(2)}) collective-permute-start(bf16[3,160,512]{2,1,0:T(8,128)(2,1)} %get-tuple-element.186), channel_id=1, source_target_pairs={{0,1},{1,0},{2,3},{3,2},{4,5},{5,4},{6,7},{7,6},{8,9},{9,8},{10,11... | collective-permute-start | bytes 1474568 | tf_op jit(solution)/shard_map/ppermute | solution.py:273
  (68 other events, 593.2 us)
Sparse Core Ops, SparseCore 0:
  30.5 38.1 all-gather.4
  75.1 36.2 all-gather.6
  176.6 52.8 reduce-scatter.2
  252.7 19.4 reduce-scatter.4
